TPU v7x, 32 devices: a whole 2x2x4 slice. The times are simulated.
32 devices in a mesh: groups: 1, frames: 32 (over z, y, x, core).
Axes of the slice: x: 2, y: 2, z: 4, core: 2. Of those that a mesh axis runs over, the one named last changes fastest.
Arguments:
- features: bfloat16 [32, 4096, 256], P(('groups', 'frames')), may hold values from -6 to 6
- query_frame: int32 [128], P('groups'), may hold values from 0 to 31
- query_pos: int32 [128], P('groups'), may hold values from 0 to 4095
- frame_order: int32 [32], P('groups'), may hold values from 0 to 31, each once
- conv1_weight: float32 [16, 9], replicated, may hold values from -2 to 2
- conv1_bias: float32 [16], replicated, may hold values from -0.5 to 0.5
- conv2_weight: bfloat16 [32, 16, 2, 2], replicated, may hold values from -0.75 to 0.75
- proj_weight: bfloat16 [2048, 512], replicated, may hold values from -0.125 to 0.125
- norm_gains: float32 [2, 2, 512], replicated, may hold values from 0.25 to 1.75
- time_kernels: float32 [2, 3, 512], replicated, may hold values from -3 to 3
- mix_up: bfloat16 [2, 512, 2048], replicated, may hold values from -0.25 to 0.25
- mix_down: bfloat16 [2, 2048, 512], replicated, may hold values from -0.125 to 0.125
Outputs:
- mixed: bfloat16 [32, 128, 512], P(('groups', 'frames'))
Inputs may be any that keep to these rules, and one draw needn't show every extreme that they name: query_pos = y * 64 + x. `frame_order`: a permutation: every time index once.
All inputs are finite; a program needn't handle non-finite values.
Results may differ from a plain program's by a relative error of at most 0.015.
Values may be sent and summed in bfloat16 or wider, within the bound.
No kernel may reach another device: no remote copies, remote signals or barrier semaphores. Data moves between devices by JAX's collectives and lax.ppermute only.
A program may use at most 128 MiB of HBM per device.

v0:
```python
import jax
import jax.numpy as jnp
from jax import lax
from jax.sharding import PartitionSpec as P

MAP = 64
CH1 = 16
CH2 = 32
GRID = 8


def layer_norm(values):
    center = values - jnp.mean(values, axis=-1, keepdims=True)
    spread = jnp.mean(center * center, axis=-1, keepdims=True)
    return center * lax.rsqrt(spread + 1e-05)


def frame_rows(feature_map, queries, conv1_weight, conv1_bias, conv2_weight, proj_weight):
    channels = feature_map.shape[1]
    count = queries.shape[0]
    corr = jnp.dot(feature_map, queries.T, preferred_element_type=jnp.float32) / jnp.sqrt(
        jnp.float32(channels)
    )
    cube = corr.reshape(MAP, MAP, count)
    padded = jnp.pad(cube, ((1, 1), (1, 1), (0, 0)))
    total = jnp.zeros((CH1, MAP, MAP, count), jnp.float32) + conv1_bias[:, None, None, None]
    for shift_y in range(3):
        for shift_x in range(3):
            window = padded[shift_y : shift_y + MAP, shift_x : shift_x + MAP, :]
            total = (
                total + conv1_weight[:, 3 * shift_y + shift_x][:, None, None, None] * window[None]
            )
    first = jax.nn.relu(total).astype(jnp.bfloat16)
    half = MAP // 2
    blocks = first.reshape(CH1, half, 2, half, 2, count)
    second = jnp.einsum(
        "cyaxbt,ocab->oyxt", blocks, conv2_weight, preferred_element_type=jnp.float32
    )
    second = jax.nn.relu(second)
    width = half // GRID
    pooled = second.reshape(CH2, GRID, width, GRID, width, count).mean(axis=(2, 4))
    pooled = pooled.reshape(CH2 * GRID * GRID, count).astype(jnp.bfloat16)
    rows = lax.dot_general(
        pooled, proj_weight, (((0,), (0,)), ((), ())), preferred_element_type=jnp.float32
    )
    return rows.astype(jnp.bfloat16)


def mix_tracks(rows, frame_order, norm_gains, time_kernels, mix_up, mix_down):
    total_frames = rows.shape[0]
    inverse = (
        jnp.zeros((total_frames,), jnp.int32)
        .at[frame_order]
        .set(jnp.arange(total_frames, dtype=jnp.int32))
    )
    state = rows[inverse].astype(jnp.float32)
    width = state.shape[-1]
    for block in range(norm_gains.shape[0]):
        normed = layer_norm(state) * norm_gains[block, 0]
        padded = jnp.pad(normed, ((1, 1), (0, 0), (0, 0)))
        state = (
            state
            + time_kernels[block, 0] * padded[:-2]
            + time_kernels[block, 1] * padded[1:-1]
            + time_kernels[block, 2] * padded[2:]
        )
        inner = (layer_norm(state) * norm_gains[block, 1]).astype(jnp.bfloat16).reshape(-1, width)
        hidden = jax.nn.gelu(
            jnp.dot(inner, mix_up[block], preferred_element_type=jnp.float32)
        ).astype(jnp.bfloat16)
        state = state + jnp.dot(
            hidden, mix_down[block], preferred_element_type=jnp.float32
        ).reshape(state.shape)
    return state[frame_order].astype(jnp.bfloat16)


def on_device(
    features,
    query_frame,
    query_pos,
    frame_order,
    conv1_weight,
    conv1_bias,
    conv2_weight,
    proj_weight,
    norm_gains,
    time_kernels,
    mix_up,
    mix_down,
):
    devices = lax.axis_size("frames")
    device_index = lax.axis_index("frames")
    local_frames = features.shape[0]
    track_count = query_frame.shape[0]
    per_device = track_count // devices
    width = proj_weight.shape[1]
    local_slot = query_frame - device_index * local_frames
    owned = (local_slot >= 0) & (local_slot < local_frames)
    safe_slot = jnp.clip(local_slot, 0, local_frames - 1)
    picked = features[safe_slot, query_pos].astype(jnp.float32)
    masked = jnp.where(owned[:, None], picked, jnp.float32(0.0))
    queries = lax.psum(masked.astype(jnp.bfloat16), "frames")
    computed = [
        frame_rows(features[0], queries, conv1_weight, conv1_bias, conv2_weight, proj_weight)
    ]
    stacked = jnp.stack(computed, axis=0).reshape(local_frames, devices, per_device, width)
    mixed_rows = mix_tracks(
        lax.all_to_all(stacked, "frames", split_axis=1, concat_axis=0, tiled=True)[:, 0],
        frame_order,
        norm_gains,
        time_kernels,
        mix_up,
        mix_down,
    )
    mixed = mixed_rows[:, None]
    returned = lax.all_to_all(mixed, "frames", split_axis=0, concat_axis=1, tiled=True)
    return returned.reshape(local_frames, track_count, width)


def solution(mesh):
    placed = (
        P(("groups", "frames"), None, None),
        P("groups"),
        P("groups"),
        P("groups"),
        P(),
        P(),
        P(),
        P(),
        P(),
        P(),
        P(),
        P(),
    )
    return jax.shard_map(
        on_device,
        mesh=mesh,
        in_specs=placed,
        out_specs=P(("groups", "frames"), None, None),
        check_vma=False,
    )
```

profile of v0, /device:TPU:0, one launch (start us, length us, event | category | flops | bytes accessed | tf_op | source)
XLA Modules:
  0.0 237.1 jit_solution(4899502808477166728)
XLA Ops:
  6.5 0.0 copy-start
  6.5 0.0 all-reduce.5.cloned.1.call-start
  6.5 0.8 compare_and_fusion
  7.4 0.7 fusion.83
  8.0 0.1 copy-done
  8.1 1.0 gather_fusion
  9.1 0.7 select_convert_fusion
  9.8 0.0 all-reduce.5.cloned.1.call-update
  9.8 1.9 slice_reduce_fusion.8
  11.7 0.7 compare_select_fusion.1
  12.4 0.7 scatter_custom_fusion
  13.1 0.5 compare_select_fusion
  13.6 1.4 fusion.92
  15.0 0.6 pad_clamp_fusion
  15.6 117.7 %all-reduce.5.cloned.1.call-done = bf16[128,256]{1,0:T(8,128)(2,1)} async-done(((bf16[128,256]{1,0:T(8,128)(2,1)}), bf16[128,256]{1,0:T(8,128)(2,1)}) %all-reduce.5.cloned.1.call-update) | async-done | bytes 65552 | tf_op jit(solution)/shard_map/psum | solution.py:102
  133.2 3.0 %fusion.21 = f32[4096,128]{0,1:T(8,128)} fusion(bf16[128,256]{1,0:T(8,128)(2,1)} %all-reduce.5.cloned.1.call-done, bf16[1,4096,256]{2,1,0:T(8,128)(2,1)S(1)} %copy-done), kind=kOutput, calls=%fused_computation.28 | convolution fusion | flops 268959744 | bytes 4259840 | tf_op jit(solution)/shard_map/dot_general | solution.py:21
  136.2 2.9 %copy.63 = f32[4096,128]{1,0:T(8,128)} copy(f32[4096,128]{0,1:T(8,128)} %fusion.21) | data formatting | bytes 4194304 | tf_op jit(solution)/shard_map/div | solution.py:21
  139.1 0.0 copy-start.1
  139.1 9.6 %pad_slice_fusion.7 = (f32[64,64,128]{2,1,0:T(8,128)S(1)}, f32[64,64,128]{2,1,0:T(8,128)S(1)}, f32[64,64,128]{2,1,0:T(8,128)S(1)}, f32[64,64,128]{2,1,0:T(8,128)...) fusion(f32[64,64,128]{2,1,0:T(8,128)} %bitcast.75), kind=kLoop, calls=%fused_computation.36 | loop fusion | bytes 18874368 | tf_op jit(solution)/shard_map/slice | solution.py:29
  148.7 0.0 copy-done.1
  148.8 33.3 %bitcast_maximum_fusion = f32[32,32,128,32]{2,3,1,0:T(8,128)} fusion(f32[16]{0:T(128)} %get-tuple-element.12, f32[16]{0:T(128)} %get-tuple-element.13, f32[16]{0:T(128)S(1)} %get-tuple-element.6, f32[16]{0:T(128)S(1)} %get-tuple-element.7, f32[16]{0:T(128)S(1)} %get-tuple-element.8, f32[16]{0:T(128)S(1)} %get-tuple-element.9, f32[16]{0:T(128)S(1)} %get-tuple-element.10, ...), kind=kOutput, calls=%fused_computation.6 | convolution fusion | flops 708837376 | bytes 35656320 | tf_op jit(solution)/shard_map/cyaxbt,ocab->oyxt/dot_general | solution.py:36
  182.0 8.0 %reduce_sum.81 = f32[32,8,8,128]{3,0,2,1:T(8,128)S(1)} reduce(f32[32,8,4,8,4,128]{5,0,4,3,2,1:T(8,128)} %bitcast.74, f32[]{:T(128)} %constant.38.clone.1), dimensions={2,4}, to_apply=%region_1.2 | reduce | flops 3932160 | bytes 17825796 | tf_op jit(solution)/shard_map/reduce_sum | solution.py:41
  190.0 0.0 copy-start.2
  190.0 0.1 multiply_convert_fusion
  190.2 0.0 copy-start.5
  190.2 0.0 copy-start.3
  190.2 0.2 copy.75
  190.4 1.2 copy-done.2
  191.6 0.5 convolution_convert_fusion
  192.1 0.7 reshape_stack.3
  192.8 5.5 %all-to-all-start = ((bf16[1,32,4,512]{3,2,0,1:T(4,128)(2,1)}), bf16[1,32,4,512]{3,2,0,1:T(4,128)(2,1)S(1)}, u32[]{:S(2)}, u32[]{:S(2)}) async-start(bf16[1,32,4,512]{3,2,0,1:T(4,128)(2,1)} %bitcast.18), calls=%async_computation | async-start | bytes 262144 | tf_op jit(solution)/shard_map/all_to_all | solution.py:108
  198.3 0.0 copy-done.5
  198.4 0.0 copy-done.3
  198.4 8.0 %all-to-all-done = bf16[1,32,4,512]{3,2,0,1:T(4,128)(2,1)S(1)} async-done(((bf16[1,32,4,512]{3,2,0,1:T(4,128)(2,1)}), bf16[1,32,4,512]{3,2,0,1:T(4,128)(2,1)S(1)}, u32[]{:S(2)}, u32[]{:S(2)}) %all-to-all-start) | async-done | bytes 131104 | tf_op jit(solution)/shard_map/all_to_all | solution.py:108
  206.4 0.7 gather_fusion.1
  207.1 0.1 convert_reduce_fusion
  207.2 0.2 fusion.69
  207.4 0.1 fusion.70
  207.5 0.2 fusion.89
  207.7 0.2 multiply_reduce_fusion.2
  207.9 0.1 multiply_convert_fusion.2
  208.0 0.1 copy.78
  208.1 2.2 fusion.50
  210.4 0.2 dot_general.29
  210.6 0.0 copy-start.4
  210.6 2.3 fusion.93
  212.9 0.2 multiply_reduce_fusion.1
  213.1 0.0 copy-done.4
  213.1 0.1 multiply_multiply_fusion.2
  213.3 0.2 fusion.87
  213.4 0.2 multiply_reduce_fusion
  213.6 0.1 multiply_convert_fusion.1
  213.8 0.1 copy.80
  213.9 2.2 fusion.62
  216.2 0.2 dot_general.32
  216.4 2.2 fusion.38
  218.6 0.1 copy.82
  218.7 0.8 gather_fusion.2
  219.5 10.0 %all_to_all.8 = bf16[32,1,4,512]{3,2,1,0:T(4,128)(2,1)S(1)} all-to-all(bf16[32,1,4,512]{3,2,1,0:T(4,128)(2,1)S(1)} %bitcast.87), channel_id=1, replica_groups=mesh['groups'=1,'frames'=32] {'frames'}, dimensions={0} | all-to-all | bytes 262144 | tf_op jit(solution)/shard_map/all_to_all | solution.py:116
  229.5 0.7 reshape.132
  (13 shorter events, 0.1 us)
Async XLA Ops:
  6.5 1.6 copy-start
  6.5 126.7 %all-reduce.5.cloned.1.call-start = ((), (), s32[]{:S(2)}) async-start(), calls=%async_computation.2 | async-start | bytes 131072 | tf_op jit(solution)/shard_map/psum | solution.py:102
  139.1 9.6 %copy-start.1 = (f32[4096,128]{1,0:T(8,128)S(1)}, f32[4096,128]{1,0:T(8,128)}, u32[]{:S(2)}) copy-start(f32[4096,128]{1,0:T(8,128)} %copy.63) | copy-start | bytes 6291460
  190.0 1.6 copy-start.2
  190.2 8.2 %copy-start.5 = (s32[32]{0:T(128)S(1)}, s32[32]{0:T(128)}, u32[]{:S(2)}) copy-start(s32[32]{0:T(128)} %compare_select_fusion) | copy-start | bytes 388
  190.2 8.2 %copy-start.3 = (f32[2,3,512]{2,0,1:T(2,128)S(1)}, f32[2,3,512]{2,0,1:T(2,128)}, u32[]{:S(2)}) copy-start(f32[2,3,512]{2,0,1:T(2,128)} %param.21) | copy-start | bytes 36868
  192.8 13.6 %all-to-all-start = ((bf16[1,32,4,512]{3,2,0,1:T(4,128)(2,1)}), bf16[1,32,4,512]{3,2,0,1:T(4,128)(2,1)S(1)}, u32[]{:S(2)}, u32[]{:S(2)}) async-start(bf16[1,32,4,512]{3,2,0,1:T(4,128)(2,1)} %bitcast.18), calls=%async_computation | async-start | bytes 262144 | tf_op jit(solution)/shard_map/all_to_all | solution.py:108
  210.6 2.5 %copy-start.4 = (f32[1,1,512]{2,1,0:T(1,128)S(1)}, f32[1,1,512]{2,1,0:T(1,128)}, u32[]{:S(2)}) copy-start(f32[1,1,512]{2,1,0:T(1,128)} %get-tuple-element.35) | copy-start | bytes 6148
Sparse Core Ops, SparseCore 0:
  12.9 120.2 all-reduce.4
where the time goes:
time: 238 us; the launch traced here: 237 us
  waiting for transfers between devices  126 us (53%)
  matrix products  45.8 us (19%)
  local copies, waits for them, and re-layouts  22.6 us (9%)
  other arithmetic  13.8 us (6%)
  between operations  13.7 us (6%)
  blocking collectives  10 us (4%)
  starting transfers between devices  5.54 us (2%)
    psum x1, waiting for transfers between devices, on_device(): queries = lax.psum(masked.astype(jnp.bfloat16), 'frames')  118 us
    dot_general x1, matrix products, frame_rows(): jnp.einsum('cyaxbt,ocab->oyxt', blocks, conv2_weight, preferred_element_t...  33.3 us
    all_to_all x1, blocking collectives, on_device(): lax.all_to_all(mixed, 'frames', split_axis=0, concat_axis=1, tiled=True)  10 us
    slice x1, local copies, waits for them, and re-layouts, frame_rows(): window = padded[shift_y:shift_y + MAP, shift_x:shift_x + MAP, :]  9.62 us
    all_to_all x1, waiting for transfers between devices, on_device(): lax.all_to_all(stacked, 'frames', split_axis=1, concat_axis=0, tiled=True)  7.99 us
    reduce_sum x1, other arithmetic, frame_rows(): second.reshape(CH2, GRID, width, GRID, width, count).mean(axis=(2, 4))  7.99 us
    all_to_all x1, starting transfers between devices, on_device(): lax.all_to_all(stacked, 'frames', split_axis=1, concat_axis=0, tiled=True)  5.54 us
  transfers between devices with their start and end apart: 2, of which 2 were waited for; matrix products, arithmetic and copies ran while one was open for 2% of the time, Pallas kernels for 0%

commit v1 on v0

v1 whole, which is shorter than its diff:
```python
import math

import jax
import jax.numpy as jnp
from jax import lax
from jax.experimental import pallas as pl
from jax.experimental.pallas import tpu as pltpu
from jax.sharding import PartitionSpec as P

AXIS = "frames"
NT = (((1,), (1,)), ((), ()))
TN = (((0,), (0,)), ((), ()))


def sum_over_frames(values, devices):
    if devices & (devices - 1):
        return lax.psum(values, AXIS)
    bit = 1
    while bit < devices:
        if bit == 1 or 2 * bit >= devices:
            shifts = (bit,)
        else:
            shifts = (bit, 2 * bit, 3 * bit)
        arrived = [
            lax.ppermute(values, AXIS, [(i, i ^ shift) for i in range(devices)])
            for shift in shifts
        ]
        for part in arrived:
            values = values + part
        bit *= len(shifts) + 1
    return values


def conv_tables(conv1_weight, conv1_bias, conv2_weight, proj_weight, side, grid):
    ch1 = conv1_weight.shape[0]
    ch2 = conv2_weight.shape[0]
    width = side // 2 // grid
    group = max(1, min(grid, 256 // (4 * ch1)))
    lanes = jnp.arange(width * grid * ch1 * 4, dtype=jnp.int32)
    col_b = lanes % 2
    row_a = (lanes // 2) % 2
    chan = (lanes // 4) % ch1
    grid_j = (lanes // (4 * ch1)) % grid
    win_s = lanes // (4 * ch1 * grid)
    at_x = 2 * (grid_j * width + win_s) + col_b
    positions = jnp.arange(4 * side, dtype=jnp.int32)
    diff = (positions // side * (4 * side) + positions % side)[:, None] - (
        row_a * (4 * side) + at_x - 1
    )[None, :]
    taps = conv1_weight.astype(jnp.bfloat16).T
    taps = jnp.broadcast_to(taps[:, None, :, None], (9, width * grid, ch1, 4)).reshape(9, -1)
    first = jnp.zeros(diff.shape, jnp.bfloat16)
    for dy in range(3):
        for dx in range(3):
            first = jnp.where(diff == dy * (4 * side) + dx, taps[3 * dy + dx][None, :], first)
    bias = jnp.broadcast_to(conv1_bias[None, :, None], (group, ch1, 4)).reshape(1, -1)
    small = conv2_weight.reshape(ch2, ch1 * 4).T
    eye = jnp.eye(group, dtype=small.dtype)
    second = (eye[:, None, :, None] * small[None, :, None, :]).reshape(
        group * ch1 * 4, group * ch2
    )
    proj = proj_weight.reshape(ch2, grid * grid, -1).transpose(1, 0, 2)
    return first, bias, second, proj.reshape(proj_weight.shape)


def rows_kernel(
    side, grid, query_ref, feat_hbm, first_ref, bias_ref, second_ref, proj_ref, out_ref,
    feat, windows, sems,
):
    half = side // 2
    width = half // grid
    count, channels = query_ref.shape
    points = side * side
    pieces = sems.shape[0]
    piece = points // pieces
    copies = [
        pltpu.make_async_copy(
            feat_hbm.at[0, pl.ds(n * piece, piece)],
            feat.at[pl.ds(side + n * piece, piece)],
            sems.at[n],
        )
        for n in range(pieces)
    ]
    for copy in copies:
        copy.start()
    edge = jnp.zeros((side, channels), feat.dtype)
    feat[pl.ds(0, side)] = edge
    feat[pl.ds(side + points, side)] = edge
    query = query_ref[...]
    scale = 1.0 / math.sqrt(channels)
    step = 2 * side
    ready = 0
    for t in range(half + 1):
        while ready < pieces and (t + 1) * step > side + ready * piece:
            copies[ready].wait()
            ready += 1
        part = lax.dot_general(
            query, feat[t * step : (t + 1) * step], NT, preferred_element_type=jnp.float32
        )
        part = (part * scale).astype(jnp.bfloat16)
        if t < half:
            windows[t, :, :step] = part
        if t > 0:
            windows[t - 1, :, step:] = part
    bias = bias_ref[...]
    second = second_ref[...]
    lanes_in, lanes_out = second.shape
    groups = first_ref.shape[1] // (width * lanes_in)

    def grid_row(i, total):
        window = windows[pl.ds(i * width, width)].reshape(width * count, 2 * step)
        sums = [None] * groups
        for s in range(width):
            for g in range(groups):
                n = s * groups + g
                one = jnp.dot(
                    window,
                    first_ref[:, n * lanes_in : (n + 1) * lanes_in],
                    preferred_element_type=jnp.float32,
                )
                one = jnp.maximum(one + bias, 0.0).astype(jnp.bfloat16)
                two = jnp.dot(one, second, preferred_element_type=jnp.float32)
                two = jnp.maximum(two, 0.0)
                for u in range(width):
                    term = two[u * count : (u + 1) * count]
                    sums[g] = term if sums[g] is None else sums[g] + term
        pooled = jnp.concatenate(sums, axis=1) * (1.0 / (width * width))
        size = groups * lanes_out
        weights = proj_ref[pl.ds(pl.multiple_of(i * size, size), size)]
        return total + jnp.dot(
            pooled.astype(jnp.bfloat16), weights, preferred_element_type=jnp.float32
        )

    total = lax.fori_loop(
        0, grid, grid_row, jnp.zeros((count, out_ref.shape[1]), jnp.float32)
    )
    out_ref[...] = total.astype(out_ref.dtype)


def frame_rows(features, queries, conv1_weight, conv1_bias, conv2_weight, proj_weight):
    points, channels = features.shape[1:]
    count = queries.shape[0]
    side = math.isqrt(points)
    grid = math.isqrt(proj_weight.shape[0] // conv2_weight.shape[0])
    first, bias, second, proj = conv_tables(
        conv1_weight, conv1_bias, conv2_weight, proj_weight, side, grid
    )
    vmem = pl.BlockSpec(memory_space=pltpu.VMEM)

    def kernel(*refs):
        rows_kernel(side, grid, *refs)

    return pl.pallas_call(
        kernel,
        out_shape=jax.ShapeDtypeStruct((count, proj.shape[1]), jnp.bfloat16),
        in_specs=[vmem, pl.BlockSpec(memory_space=pl.ANY), vmem, vmem, vmem, vmem],
        out_specs=vmem,
        scratch_shapes=[
            pltpu.VMEM((points + 2 * side, channels), jnp.bfloat16),
            pltpu.VMEM((side // 2, count, 4 * side), jnp.bfloat16),
            pltpu.SemaphoreType.DMA((4,)),
        ],
        compiler_params=pltpu.CompilerParams(vmem_limit_bytes=32 * 1024 * 1024),
        name="frame_rows",
    )(queries, features, first, bias, second, proj)


def layer_norm(values):
    center = values - jnp.mean(values, axis=-1, keepdims=True)
    spread = jnp.mean(center * center, axis=-1, keepdims=True)
    return center * lax.rsqrt(spread + 1e-05)


def mixer_kernel(tracks, rows_ref, place_ref, gain_ref, time_ref, up_ref, down_ref, out_ref):
    length = rows_ref.shape[0]
    slots = lax.broadcasted_iota(jnp.int32, (length, length), 0)
    order = (slots == place_ref[...]).astype(jnp.bfloat16)
    state = jnp.dot(order, rows_ref[...], preferred_element_type=jnp.float32)
    edge = jnp.zeros((tracks, state.shape[1]), jnp.float32)
    hidden_size = up_ref.shape[2]
    chunk = min(512, hidden_size)
    for block in range(up_ref.shape[0]):
        normed = layer_norm(state) * gain_ref[block, 0:1]
        before = jnp.concatenate([edge, normed[:-tracks]], axis=0)
        after = jnp.concatenate([normed[tracks:], edge], axis=0)
        state = (
            state
            + time_ref[block, 0:1] * before
            + time_ref[block, 1:2] * normed
            + time_ref[block, 2:3] * after
        )
        inner = (layer_norm(state) * gain_ref[block, 1:2]).astype(jnp.bfloat16)
        for c in range(0, hidden_size, chunk):
            hidden = jnp.dot(
                inner, up_ref[block, :, c : c + chunk], preferred_element_type=jnp.float32
            )
            hidden = jax.nn.gelu(hidden, approximate=True).astype(jnp.bfloat16)
            state = state + jnp.dot(
                hidden, down_ref[block, c : c + chunk, :], preferred_element_type=jnp.float32
            )
    out_ref[...] = lax.dot_general(
        order, state.astype(jnp.bfloat16), TN, preferred_element_type=jnp.float32
    ).astype(out_ref.dtype)


def mix_tracks(rows, frame_order, norm_gains, time_kernels, mix_up, mix_down, tracks):
    place = (frame_order[:, None] * tracks + jnp.arange(tracks, dtype=jnp.int32)).reshape(1, -1)
    vmem = pl.BlockSpec(memory_space=pltpu.VMEM)

    def kernel(*refs):
        mixer_kernel(tracks, *refs)

    return pl.pallas_call(
        kernel,
        out_shape=jax.ShapeDtypeStruct(rows.shape, rows.dtype),
        in_specs=[vmem] * 6,
        out_specs=vmem,
        compiler_params=pltpu.CompilerParams(vmem_limit_bytes=32 * 1024 * 1024),
        name="mixer",
    )(rows, place, norm_gains, time_kernels, mix_up, mix_down)


def on_device(
    features,
    query_frame,
    query_pos,
    frame_order,
    conv1_weight,
    conv1_bias,
    conv2_weight,
    proj_weight,
    norm_gains,
    time_kernels,
    mix_up,
    mix_down,
):
    devices = lax.axis_size(AXIS)
    track_count = query_frame.shape[0]
    per_device = track_count // devices
    owned = query_frame == lax.axis_index(AXIS)
    picked = jnp.where(owned[:, None], features[0, query_pos], jnp.bfloat16(0.0))
    queries = sum_over_frames(picked, devices)
    rows = frame_rows(features, queries, conv1_weight, conv1_bias, conv2_weight, proj_weight)
    rows = lax.all_to_all(rows, AXIS, split_axis=0, concat_axis=0, tiled=True)
    mixed = mix_tracks(
        rows, frame_order, norm_gains, time_kernels, mix_up, mix_down, per_device
    )
    mixed = lax.all_to_all(mixed, AXIS, split_axis=0, concat_axis=0, tiled=True)
    return mixed[None]


def solution(mesh):
    placed = (
        P(("groups", "frames"), None, None),
        P("groups"),
        P("groups"),
        P("groups"),
        P(),
        P(),
        P(),
        P(),
        P(),
        P(),
        P(),
        P(),
    )
    return jax.shard_map(
        on_device,
        mesh=mesh,
        in_specs=placed,
        out_specs=P(("groups", "frames"), None, None),
        check_vma=False,
    )
```

time: 238 us -> 75.4 us (0.32)
  waiting for transfers between devices: 126 us -> 15.7 us
  matrix products: 45.8 us -> 0 us
  Pallas kernels: 0 us -> 17.2 us
  between operations: 13.7 us -> 0.26 us
  other arithmetic: 13.8 us -> 4.7 us
  local copies, waits for them, and re-layouts: 22.6 us -> 15.5 us
  starting transfers between devices: 5.54 us -> 11.7 us
    psum x1 -> x0, waiting for transfers between devices: 118 us -> none  [on_device(): queries = lax.psum(masked.astype(jnp.bfloat16), 'frames')]
    dot_general x7 -> x0, matrix products: 45.8 us -> none  [the longest x1 33.3 us: frame_rows(): jnp.einsum('cyaxbt,ocab->oyxt', blocks, conv2_weight, preferred_element_t...]
    pallas_call x0 -> x2, Pallas kernels: none -> 17.2 us  [the longest x1 13.5 us: frame_rows(): pl.pallas_call(kernel, out_shape=jax.ShapeDtypeStruct((count, proj.shape[...]
    slice x4 -> x1, local copies, waits for them, and re-layouts: 12.9 us -> 0.26 us  [conv_tables(): taps[3 * dy + dx][None, :]]
    reduce_sum x8 -> x0, other arithmetic: 9.18 us -> none  [the longest x1 7.99 us: frame_rows(): second.reshape(CH2, GRID, width, GRID, width, count).mean(axis=(2, 4))]
    ppermute x0 -> x7, starting transfers between devices: none -> 9.09 us  [sum_over_frames(): lax.ppermute(values, AXIS, [(i, i ^ shift) for i in range(devices)])]
    ppermute x0 -> x7, waiting for transfers between devices: none -> 7.72 us  [sum_over_frames(): lax.ppermute(values, AXIS, [(i, i ^ shift) for i in range(devices)])]
    unnamed x12 -> x17, local copies, waits for them, and re-layouts: 1.36 us -> 5.98 us
  transfers between devices with their start and end apart: 2 -> 8, of which waited for: 2 -> 6; matrix products, arithmetic and copies ran while one was open for 2% -> 11% of each run, Pallas kernels for 0% -> 0%
where the time goes in v1:
time: 75.4 us; the launch traced here: 75 us
  Pallas kernels  17.2 us (23%)
  waiting for transfers between devices  15.7 us (21%)
  local copies, waits for them, and re-layouts  15.5 us (21%)
  starting transfers between devices  11.7 us (16%)
  blocking collectives  9.93 us (13%)
  other arithmetic  4.7 us (6%)
    pallas_call x1, Pallas kernels, frame_rows(): pl.pallas_call(kernel, out_shape=jax.ShapeDtypeStruct((count, proj.shape[...  13.5 us
    all_to_all x1, blocking collectives, on_device(): mixed = lax.all_to_all(mixed, AXIS, split_axis=0, concat_axis=0, tiled=True)  9.93 us
    ppermute x7, starting transfers between devices, sum_over_frames(): lax.ppermute(values, AXIS, [(i, i ^ shift) for i in range(devices)])  9.09 us
    all_to_all x1, waiting for transfers between devices, on_device(): rows = lax.all_to_all(rows, AXIS, split_axis=0, concat_axis=0, tiled=True)  8 us
    ppermute x7, waiting for transfers between devices, sum_over_frames(): lax.ppermute(values, AXIS, [(i, i ^ shift) for i in range(devices)])  7.72 us
    unnamed x17, local copies, waits for them, and re-layouts  5.98 us
    pallas_call x1, Pallas kernels, mix_tracks(): pl.pallas_call(kernel, out_shape=jax.ShapeDtypeStruct(rows.shape, rows.dt...  3.67 us
    reshape x1, local copies, waits for them, and re-layouts, conv_tables(): proj = proj_weight.reshape(ch2, grid * grid, -1).transpose(1, 0, 2)  2.76 us
  transfers between devices with their start and end apart: 8, of which 6 were waited for; matrix products, arithmetic and copies ran while one was open for 11% of the time, Pallas kernels for 0%

profile of v1, /device:TPU:0, one launch (start us, length us, event | category | flops | bytes accessed | tf_op | source)
XLA Modules:
  0.0 75.0 jit_solution(4295746599915282888)
XLA Ops:
  0.0 0.7 fusion.35
  0.7 2.0 %gather_fusion = bf16[128,256]{1,0:T(8,128)(2,1)S(1)} fusion(bf16[1,4096,256]{2,1,0:T(8,128)(2,1)} %refs_1_.1, s32[128]{0:T(128)S(1)} %fusion.35), kind=kCustom, calls=%fused_computation | custom fusion | bytes 132096 | tf_op jit(solution)/shard_map/gather | solution.py:241
  2.7 0.7 broadcast_compare_fusion
  3.3 0.1 broadcast_select_fusion
  3.4 0.5 collective-permute-start
  3.9 0.7 convert_bitcast_fusion
  4.6 0.3 slice_reduce_fusion.8
  4.9 0.1 broadcast_in_dim.126
  5.0 0.2 broadcast_in_dim.127
  5.2 0.1 broadcast_in_dim.129
  5.3 0.2 broadcast_in_dim.130
  5.5 0.1 broadcast_in_dim.132
  5.6 0.2 broadcast_in_dim.133
  5.8 0.1 broadcast_in_dim.135
  5.8 0.2 broadcast_in_dim.136
  6.0 0.1 broadcast_in_dim.138
  6.1 0.2 broadcast_in_dim.139
  6.3 0.1 broadcast_in_dim.141
  6.4 0.2 broadcast_in_dim.142
  6.6 0.1 broadcast_in_dim.144
  6.7 0.2 broadcast_in_dim.145
  6.9 0.1 broadcast_in_dim.147
  7.0 0.2 broadcast_in_dim.148
  7.2 0.1 broadcast_in_dim.150
  7.3 0.2 broadcast_in_dim.151
  7.4 1.4 %fusion.refs_2_ = bf16[256,2048]{1,0:T(8,128)(2,1)S(1)} fusion(s32[2048]{0:T(1024)S(1)} %fusion.18, s32[256]{0:T(256)S(1)} %fusion.32, bf16[2048]{0:T(1024)(128)(2,1)S(1)} %broadcast_in_dim.151, bf16[2048]{0:T(1024)(128)(2,1)S(1)} %broadcast_in_dim.148, bf16[2048]{0:T(1024)(128)(2,1)S(1)} %broadcast_in_dim.145, bf16[2048]{0:T(1024)(128)(2,1)S(1)} %broadcast_in_dim.142, ...), kind=kLoop, calls=%fused_computation.10 | loop fusion | flops 9961472 | bytes 1094656 | tf_op jit(solution)/shard_map/jit(_where)/select_n | solution.py:55
  8.9 0.1 copy.15
  9.0 0.0 collective-permute-done
  9.0 0.1 fusion.36
  9.1 2.6 %collective-permute-start.1 = (bf16[128,256]{1,0:T(8,128)(2,1)S(1)}, bf16[128,256]{1,0:T(8,128)(2,1)S(1)}, u32[]{:S(2)}, u32[]{:S(2)}) collective-permute-start(bf16[128,256]{1,0:T(8,128)(2,1)S(1)} %fusion.36), channel_id=1, source_target_pairs={{0,2},{1,3},{2,0},{3,1},{4,6},{5,7},{6,4},{7,5},{8,10},{9,11},{10,... | collective-permute-start | bytes 196616 | tf_op jit(solution)/shard_map/ppermute | solution.py:25
  11.6 1.5 %collective-permute-start.2 = (bf16[128,256]{1,0:T(8,128)(2,1)S(1)}, bf16[128,256]{1,0:T(8,128)(2,1)S(1)}, u32[]{:S(2)}, u32[]{:S(2)}) collective-permute-start(bf16[128,256]{1,0:T(8,128)(2,1)S(1)} %fusion.36), channel_id=1, source_target_pairs={{0,4},{1,5},{2,6},{3,7},{4,0},{5,1},{6,2},{7,3},{8,12},{9,13},{10,... | collective-permute-start | bytes 196616 | tf_op jit(solution)/shard_map/ppermute | solution.py:25
  13.2 0.0 collective-permute-start.3
  13.2 1.2 %collective-permute-done.1 = bf16[128,256]{1,0:T(8,128)(2,1)S(1)} collective-permute-done((bf16[128,256]{1,0:T(8,128)(2,1)S(1)}, bf16[128,256]{1,0:T(8,128)(2,1)S(1)}, u32[]{:S(2)}, u32[]{:S(2)}) %collective-permute-start.1) | collective-permute-done | bytes 65568 | tf_op jit(solution)/shard_map/ppermute | solution.py:25
  14.4 1.5 %collective-permute-done.2 = bf16[128,256]{1,0:T(8,128)(2,1)S(1)} collective-permute-done((bf16[128,256]{1,0:T(8,128)(2,1)S(1)}, bf16[128,256]{1,0:T(8,128)(2,1)S(1)}, u32[]{:S(2)}, u32[]{:S(2)}) %collective-permute-start.2) | collective-permute-done | bytes 65568 | tf_op jit(solution)/shard_map/ppermute | solution.py:25
  15.9 2.4 %collective-permute-done.3 = bf16[128,256]{1,0:T(8,128)(2,1)S(1)} collective-permute-done((bf16[128,256]{1,0:T(8,128)(2,1)S(1)}, bf16[128,256]{1,0:T(8,128)(2,1)S(1)}, u32[]{:S(2)}, u32[]{:S(2)}) %collective-permute-start.3) | collective-permute-done | bytes 65568 | tf_op jit(solution)/shard_map/ppermute | solution.py:25
  18.3 1.6 %collective-permute-start.4 = (bf16[128,256]{1,0:T(8,128)(2,1)S(1)}, bf16[128,256]{1,0:T(8,128)(2,1)S(1)}, u32[]{:S(2)}, u32[]{:S(2)}) collective-permute-start(bf16[128,256]{1,0:T(8,128)(2,1)S(1)} %add_add_fusion.1), channel_id=1, source_target_pairs={{0,8},{1,9},{2,10},{3,11},{4,12},{5,13},{6,14},{7,15},{8,0},{9,1},... | collective-permute-start | bytes 196616 | tf_op jit(solution)/shard_map/ppermute | solution.py:25
  20.0 2.6 %collective-permute-start.5 = (bf16[128,256]{1,0:T(8,128)(2,1)S(1)}, bf16[128,256]{1,0:T(8,128)(2,1)S(1)}, u32[]{:S(2)}, u32[]{:S(2)}) collective-permute-start(bf16[128,256]{1,0:T(8,128)(2,1)S(1)} %add_add_fusion.1), channel_id=1, source_target_pairs={{0,16},{1,17},{2,18},{3,19},{4,20},{5,21},{6,22},{7,23},{8,24},{9,... | collective-permute-start | bytes 196616 | tf_op jit(solution)/shard_map/ppermute | solution.py:25
  22.6 0.2 collective-permute-start.6
  22.8 0.1 broadcast_multiply_fusion
  22.9 0.0 copy-start.6
  22.9 2.8 %copy.16 = bf16[32,64,512]{2,0,1:T(8,128)(2,1)S(1)} copy(bf16[32,64,512]{2,1,0:T(8,128)(2,1)} %bitcast.12) | data formatting | bytes 4194304 | tf_op jit(solution)/shard_map/reshape | solution.py:62
  25.7 0.1 mul.136
  25.8 0.1 copy.17.refs_4_
  26.0 0.1 broadcast_in_dim.154
  26.0 0.1 reshape.182.refs_3_
  26.1 0.0 collective-permute-done.4
  26.2 0.4 collective-permute-done.5
  26.6 2.2 %collective-permute-done.6 = bf16[128,256]{1,0:T(8,128)(2,1)} collective-permute-done((bf16[128,256]{1,0:T(8,128)(2,1)S(1)}, bf16[128,256]{1,0:T(8,128)(2,1)}, u32[]{:S(2)}, u32[]{:S(2)}) %collective-permute-start.6) | collective-permute-done | bytes 65568 | tf_op jit(solution)/shard_map/ppermute | solution.py:25
  28.7 0.9 %add_add_fusion.refs_0_ = bf16[128,256]{1,0:T(8,128)(2,1)S(1)} fusion(bf16[128,256]{1,0:T(8,128)(2,1)} %collective-permute-done.6, bf16[128,256]{1,0:T(8,128)(2,1)S(1)} %collective-permute-done.5, bf16[128,256]{1,0:T(8,128)(2,1)S(1)} %add_add_fusion.1, bf16[128,256]{1,0:T(8,128)(2,1)S(1)} %collective-permute-done.4), kind=kLoop, calls=%fused_computation.20 | loop fusion | flops 98304 | bytes 327680 | tf_op jit(solution)/shard_map/add | solution.py:29
  29.6 0.0 copy-start.2
  29.6 1.6 %copy-done.2 = bf16[1,4096,256]{2,1,0:T(8,128)(2,1)S(1)} copy-done((bf16[1,4096,256]{2,1,0:T(8,128)(2,1)S(1)}, bf16[1,4096,256]{2,1,0:T(8,128)(2,1)}, u32[]{:S(2)}) %copy-start.2) | copy-done | bytes 2097176
  31.2 13.5 %frame_rows.1 = bf16[128,512]{1,0:T(8,128)(2,1)S(1)} custom-call(bf16[128,256]{1,0:T(8,128)(2,1)S(1)} %add_add_fusion.refs_0_, bf16[1,4096,256]{2,1,0:T(8,128)(2,1)S(1)} %copy-done.2, bf16[256,2048]{1,0:T(8,128)(2,1)S(1)} %fusion.refs_2_, f32[1,256]{1,0:T(1,128)S(1)} %reshape.182.refs_3_, bf16[256,128]{1,0:T(8,128)(2,1)S(1)} %copy.17.refs_4_, ...), custom_call_target="tpu_custom_call" | custom-call | tf_op jit(solution)/shard_map/frame_rows/pallas_call | solution.py:153
  44.7 0.7 all_to_all.13
  45.4 2.6 %all-to-all-start = ((bf16[32,4,512]{2,1,0:T(4,128)(2,1)}), bf16[32,4,512]{2,1,0:T(4,128)(2,1)S(1)}, u32[]{:S(2)}, u32[]{:S(2)}) async-start(bf16[32,4,512]{2,1,0:T(4,128)(2,1)} %all_to_all.13), calls=%async_computation | async-start | bytes 262144 | tf_op jit(solution)/shard_map/all_to_all | solution.py:244
  48.0 0.0 copy-done.7
  48.0 0.1 iota_add_fusion
  48.1 0.1 add.289.refs_1_
  48.2 8.0 %all-to-all-done = bf16[32,4,512]{2,1,0:T(4,128)(2,1)S(1)} async-done(((bf16[32,4,512]{2,1,0:T(4,128)(2,1)}), bf16[32,4,512]{2,1,0:T(4,128)(2,1)S(1)}, u32[]{:S(2)}, u32[]{:S(2)}) %all-to-all-start) | async-done | bytes 131104 | tf_op jit(solution)/shard_map/all_to_all | solution.py:244
  56.3 0.0 copy-start
  56.3 2.2 %copy-done = bf16[2,512,2048]{2,1,0:T(8,128)(2,1)S(1)} copy-done((bf16[2,512,2048]{2,1,0:T(8,128)(2,1)S(1)}, bf16[2,512,2048]{2,1,0:T(8,128)(2,1)}, u32[]{:S(2)}) %copy-start) | copy-done | bytes 4194328
  58.5 2.2 %copy-done.1 = bf16[2,2048,512]{2,1,0:T(8,128)(2,1)S(1)} copy-done((bf16[2,2048,512]{2,1,0:T(8,128)(2,1)S(1)}, bf16[2,2048,512]{2,1,0:T(8,128)(2,1)}, u32[]{:S(2)}) %copy-start.1) | copy-done | bytes 4194328
  60.6 3.7 %mixer.1 = bf16[128,512]{1,0:T(8,128)(2,1)S(1)} custom-call(bf16[128,512]{1,0:T(8,128)(2,1)S(1)} %all_to_all.15.refs_0_, s32[1,128]{1,0:T(1,128)S(1)} %add.289.refs_1_, f32[2,2,512]{2,1,0:T(2,128)S(1)} %copy-done.3, f32[2,3,512]{2,1,0:T(4,128)S(1)} %copy.18.refs_3_, bf16[2,512,2048]{2,1,0:T(8,128)(2,1)S(1)} %copy-done, bf16[2,2048,512]{2,1,0:T(8,128)(2,1)S(1)} %copy-done.1), custom_call_target="tpu_custom_call" | custom-call | tf_op jit(solution)/shard_map/mixer/pallas_call | solution.py:213
  64.4 9.9 %all_to_all.20 = bf16[32,4,512]{2,1,0:T(4,128)(2,1)S(1)} all-to-all(bf16[32,4,512]{2,1,0:T(4,128)(2,1)S(1)} %all_to_all.16), channel_id=1, replica_groups=mesh['groups'=1,'frames'=32] {'frames'}, dimensions={0} | all-to-all | bytes 262144 | tf_op jit(solution)/shard_map/all_to_all | solution.py:248
  74.3 0.7 broadcast_in_dim.155
  (17 shorter events, 0.1 us)
Async XLA Ops:
  0.7 8.2 %copy-start.4 = (bf16[32,16,2,2]{0,3,2,1:T(2,128)(2,1)S(1)}, bf16[32,16,2,2]{0,3,2,1:T(2,128)(2,1)}, u32[]{:S(2)}) copy-start(bf16[32,16,2,2]{0,3,2,1:T(2,128)(2,1)} %param.18) | copy-start | bytes 12292
  3.4 5.5 %collective-permute-start = (bf16[128,256]{1,0:T(8,128)(2,1)S(1)}, bf16[128,256]{1,0:T(8,128)(2,1)S(1)}, u32[]{:S(2)}, u32[]{:S(2)}) collective-permute-start(bf16[128,256]{1,0:T(8,128)(2,1)S(1)} %broadcast_select_fusion), channel_id=1, source_target_pairs={{0,1},{1,0},{2,3},{3,2},{4,5},{5,4},{6,7},{7,6},{8,9},{9,8},{10,11... | collective-permute-start | bytes 196616 | tf_op jit(solution)/shard_map/ppermute | solution.py:25
  9.1 5.3 %collective-permute-start.1 = (bf16[128,256]{1,0:T(8,128)(2,1)S(1)}, bf16[128,256]{1,0:T(8,128)(2,1)S(1)}, u32[]{:S(2)}, u32[]{:S(2)}) collective-permute-start(bf16[128,256]{1,0:T(8,128)(2,1)S(1)} %fusion.36), channel_id=1, source_target_pairs={{0,2},{1,3},{2,0},{3,1},{4,6},{5,7},{6,4},{7,5},{8,10},{9,11},{10,... | collective-permute-start | bytes 196616 | tf_op jit(solution)/shard_map/ppermute | solution.py:25
  11.6 4.3 %collective-permute-start.2 = (bf16[128,256]{1,0:T(8,128)(2,1)S(1)}, bf16[128,256]{1,0:T(8,128)(2,1)S(1)}, u32[]{:S(2)}, u32[]{:S(2)}) collective-permute-start(bf16[128,256]{1,0:T(8,128)(2,1)S(1)} %fusion.36), channel_id=1, source_target_pairs={{0,4},{1,5},{2,6},{3,7},{4,0},{5,1},{6,2},{7,3},{8,12},{9,13},{10,... | collective-permute-start | bytes 196616 | tf_op jit(solution)/shard_map/ppermute | solution.py:25
  13.2 5.2 %collective-permute-start.3 = (bf16[128,256]{1,0:T(8,128)(2,1)S(1)}, bf16[128,256]{1,0:T(8,128)(2,1)S(1)}, u32[]{:S(2)}, u32[]{:S(2)}) collective-permute-start(bf16[128,256]{1,0:T(8,128)(2,1)S(1)} %fusion.36), channel_id=1, source_target_pairs={{0,6},{1,7},{2,4},{3,5},{4,2},{5,3},{6,0},{7,1},{8,14},{9,15},{10,... | collective-permute-start | bytes 196616 | tf_op jit(solution)/shard_map/ppermute | solution.py:25
  18.3 7.8 %collective-permute-start.4 = (bf16[128,256]{1,0:T(8,128)(2,1)S(1)}, bf16[128,256]{1,0:T(8,128)(2,1)S(1)}, u32[]{:S(2)}, u32[]{:S(2)}) collective-permute-start(bf16[128,256]{1,0:T(8,128)(2,1)S(1)} %add_add_fusion.1), channel_id=1, source_target_pairs={{0,8},{1,9},{2,10},{3,11},{4,12},{5,13},{6,14},{7,15},{8,0},{9,1},... | collective-permute-start | bytes 196616 | tf_op jit(solution)/shard_map/ppermute | solution.py:25
  20.0 6.6 %collective-permute-start.5 = (bf16[128,256]{1,0:T(8,128)(2,1)S(1)}, bf16[128,256]{1,0:T(8,128)(2,1)S(1)}, u32[]{:S(2)}, u32[]{:S(2)}) collective-permute-start(bf16[128,256]{1,0:T(8,128)(2,1)S(1)} %add_add_fusion.1), channel_id=1, source_target_pairs={{0,16},{1,17},{2,18},{3,19},{4,20},{5,21},{6,22},{7,23},{8,24},{9,... | collective-permute-start | bytes 196616 | tf_op jit(solution)/shard_map/ppermute | solution.py:25
  22.6 6.2 %collective-permute-start.6 = (bf16[128,256]{1,0:T(8,128)(2,1)S(1)}, bf16[128,256]{1,0:T(8,128)(2,1)}, u32[]{:S(2)}, u32[]{:S(2)}) collective-permute-start(bf16[128,256]{1,0:T(8,128)(2,1)S(1)} %add_add_fusion.1), channel_id=1, source_target_pairs={{0,24},{1,25},{2,26},{3,27},{4,28},{5,29},{6,30},{7,31},{8,16},{9,... | collective-permute-start | bytes 196616 | tf_op jit(solution)/shard_map/ppermute | solution.py:25
  22.9 3.0 %copy-start.6 = (f32[16]{0:T(128)S(1)}, f32[16]{0:T(128)}, u32[]{:S(2)}) copy-start(f32[16]{0:T(128)} %param.17) | copy-start | bytes 196
  29.6 1.6 %copy-start.2 = (bf16[1,4096,256]{2,1,0:T(8,128)(2,1)S(1)}, bf16[1,4096,256]{2,1,0:T(8,128)(2,1)}, u32[]{:S(2)}) copy-start(bf16[1,4096,256]{2,1,0:T(8,128)(2,1)} %refs_1_.1) | copy-start | bytes 6291460
  31.2 16.8 %copy-start.7 = (s32[32]{0:T(128)S(1)}, s32[32]{0:T(128)}, u32[]{:S(2)}) copy-start(s32[32]{0:T(128)} %param.15) | copy-start | bytes 388
  31.2 17.0 %copy-start.5 = (f32[2,3,512]{2,0,1:T(2,128)S(1)}, f32[2,3,512]{2,0,1:T(2,128)}, u32[]{:S(2)}) copy-start(f32[2,3,512]{2,0,1:T(2,128)} %param.21) | copy-start | bytes 36868
  31.2 25.1 %copy-start.3 = (f32[2,2,512]{2,1,0:T(2,128)S(1)}, f32[2,2,512]{2,1,0:T(2,128)}, u32[]{:S(2)}) copy-start(f32[2,2,512]{2,1,0:T(2,128)} %refs_2_.1) | copy-start | bytes 24580
  45.4 10.8 %all-to-all-start = ((bf16[32,4,512]{2,1,0:T(4,128)(2,1)}), bf16[32,4,512]{2,1,0:T(4,128)(2,1)S(1)}, u32[]{:S(2)}, u32[]{:S(2)}) async-start(bf16[32,4,512]{2,1,0:T(4,128)(2,1)} %all_to_all.13), calls=%async_computation | async-start | bytes 262144 | tf_op jit(solution)/shard_map/all_to_all | solution.py:244
  56.3 2.2 %copy-start = (bf16[2,512,2048]{2,1,0:T(8,128)(2,1)S(1)}, bf16[2,512,2048]{2,1,0:T(8,128)(2,1)}, u32[]{:S(2)}) copy-start(bf16[2,512,2048]{2,1,0:T(8,128)(2,1)} %refs_4_.1) | copy-start | bytes 12582916
  58.5 2.2 %copy-start.1 = (bf16[2,2048,512]{2,1,0:T(8,128)(2,1)S(1)}, bf16[2,2048,512]{2,1,0:T(8,128)(2,1)}, u32[]{:S(2)}) copy-start(bf16[2,2048,512]{2,1,0:T(8,128)(2,1)} %refs_5_.1) | copy-start | bytes 12582916

commit v2 on v1

v2 whole, which is shorter than its diff:
```python
import math

import jax
import jax.numpy as jnp
from jax import lax
from jax.experimental import pallas as pl
from jax.experimental.pallas import tpu as pltpu
from jax.sharding import PartitionSpec as P

AXIS = "frames"
NT = (((1,), (1,)), ((), ()))
TN = (((0,), (0,)), ((), ()))
VMEM = pl.BlockSpec(memory_space=pltpu.VMEM)
HBM = pl.BlockSpec(memory_space=pltpu.HBM)
MIB = 1024 * 1024


def iota(shape, axis):
    return lax.broadcasted_iota(jnp.int32, shape, axis)


def exchange_stages(devices):
    stages = []
    bit = 1
    while bit < devices:
        if bit == 1 or 2 * bit >= devices:
            stages.append((bit,))
        else:
            stages.append((bit, 2 * bit, 3 * bit))
        bit *= len(stages[-1]) + 1
    return stages


def exchange(values, shifts, devices):
    arrived = [
        lax.ppermute(values, AXIS, [(i, i ^ shift) for i in range(devices)]) for shift in shifts
    ]
    for part in arrived:
        values = values + part
    return values


def pick_kernel(pieces, wanted_ref, feat_hbm, out_ref, feat, sems):
    points, channels = feat.shape
    count = wanted_ref.shape[1]
    piece = points // pieces
    copies = [
        pltpu.make_async_copy(
            feat_hbm.at[0, pl.ds(n * piece, piece)], feat.at[pl.ds(n * piece, piece)], sems.at[n]
        )
        for n in range(pieces)
    ]
    for copy in copies:
        copy.start()
    wanted = jnp.broadcast_to(wanted_ref[...], (count, count)).T
    total = jnp.zeros((count, channels), jnp.float32)
    for n in range(pieces):
        parts = []
        for at in range(n * piece, (n + 1) * piece, count):
            parts.append((wanted == iota((count, count), 1) + at).astype(jnp.bfloat16))
        hot = jnp.concatenate(parts, axis=1)
        copies[n].wait()
        total = total + jnp.dot(
            hot, feat[n * piece : (n + 1) * piece], preferred_element_type=jnp.float32
        )
    out_ref[...] = total.astype(out_ref.dtype)


def pick_queries(features, query_frame, query_pos):
    points, channels = features.shape[1:]
    count = query_frame.shape[0]
    wanted = jnp.where(query_frame == lax.axis_index(AXIS), query_pos, -1)
    pieces = 4

    def kernel(*refs):
        pick_kernel(pieces, *refs)

    return pl.pallas_call(
        kernel,
        out_shape=jax.ShapeDtypeStruct((count, channels), features.dtype),
        in_specs=[VMEM, HBM],
        out_specs=VMEM,
        scratch_shapes=[
            pltpu.VMEM((points, channels), features.dtype),
            pltpu.SemaphoreType.DMA((pieces,)),
        ],
        compiler_params=pltpu.CompilerParams(vmem_limit_bytes=53 * MIB),
        name="pick_queries",
    )(wanted.reshape(1, -1), features)


def tables_kernel(
    side, grid, taps_ref, bias_ref, small_ref, first_ref, lane_bias_ref, second_ref
):
    ch1, ch2 = taps_ref.shape[0], small_ref.shape[1]
    width = side // 2 // grid
    lanes = grid * ch1 * 4
    rows = 4 * side
    lane = iota((1, lanes), 1)
    hot = (iota((ch1, lanes), 0) == iota((ch1, lanes), 1) // 4 % ch1).astype(jnp.float32)
    lane_bias_ref[...] = jnp.dot(
        bias_ref[...], hot, precision=lax.Precision.HIGHEST, preferred_element_type=jnp.float32
    )
    taps = lax.dot_general(
        taps_ref[...].astype(jnp.bfloat16),
        hot.astype(jnp.bfloat16),
        TN,
        preferred_element_type=jnp.float32,
    )
    at = lane // 2 % 2 * rows + 2 * width * (lane // (4 * ch1)) + lane % 2 - 1
    spot = iota((rows, 1), 0)
    diff = spot // side * rows + spot % side - at
    for s in range(width):
        first = jnp.zeros((rows, lanes), jnp.float32)
        for dy in range(3):
            for dx in range(3):
                n = 3 * dy + dx
                first = jnp.where(diff == dy * rows + dx + 2 * s, taps[n : n + 1], first)
        first_ref[:, s * lanes : (s + 1) * lanes] = first.astype(jnp.bfloat16)

    out_lanes = ch2 * grid
    hot = (iota((ch2, out_lanes), 0) == iota((ch2, out_lanes), 1) // grid).astype(jnp.bfloat16)
    wide = jnp.dot(small_ref[...], hot, preferred_element_type=jnp.float32)
    for j in range(grid):
        second_ref[j * 4 * ch1 : (j + 1) * 4 * ch1] = jnp.where(
            iota(wide.shape, 1) % grid == j, wide, 0.0
        ).astype(jnp.bfloat16)


def conv_tables(conv1_weight, conv1_bias, conv2_weight, side, grid):
    ch1 = conv1_weight.shape[0]
    ch2 = conv2_weight.shape[0]
    lanes = grid * ch1 * 4

    def kernel(*refs):
        tables_kernel(side, grid, *refs)

    return pl.pallas_call(
        kernel,
        out_shape=[
            jax.ShapeDtypeStruct((4 * side, side // 2 // grid * lanes), jnp.bfloat16),
            jax.ShapeDtypeStruct((1, lanes), jnp.float32),
            jax.ShapeDtypeStruct((lanes, ch2 * grid), jnp.bfloat16),
        ],
        in_specs=[VMEM] * 3,
        out_specs=[VMEM] * 3,
        compiler_params=pltpu.CompilerParams(vmem_limit_bytes=24 * MIB),
        name="conv_tables",
    )(conv1_weight, conv1_bias.reshape(1, ch1), conv2_weight.transpose(1, 2, 3, 0).reshape(ch1 * 4, ch2))


def rows_kernel(
    side, grid, query_ref, feat_ref, first_ref, bias_ref, second_ref, proj_ref, out_ref, windows, sums
):
    half = side // 2
    width = half // grid
    count, channels = query_ref.shape
    query = query_ref[...]
    scale = 1.0 / math.sqrt(channels)
    step = 2 * side
    for t in range(half + 1):
        part = lax.dot_general(
            query, feat_ref[t * step : (t + 1) * step], NT, preferred_element_type=jnp.float32
        )
        part = (part * scale).astype(jnp.bfloat16)
        if t < half:
            windows[t, :, :step] = part
        if t > 0:
            windows[t - 1, :, step:] = part
    bias = bias_ref[...]
    lanes_in, lanes_out = second_ref.shape
    for s in range(width):
        for i in range(grid):
            window = windows[i * width : (i + 1) * width].reshape(width * count, 2 * step)
            one = jnp.dot(
                window,
                first_ref[:, s * lanes_in : (s + 1) * lanes_in],
                preferred_element_type=jnp.float32,
            )
            one = jnp.maximum(one + bias, 0.0).astype(jnp.bfloat16)
            two = jnp.dot(one, second_ref[...], preferred_element_type=jnp.float32)
            two = jnp.maximum(two, 0.0).reshape(width, count, lanes_out)
            summed = two[0]
            for u in range(1, width):
                summed = summed + two[u]
            sums[i] = summed if s == 0 else sums[i] + summed
    total = jnp.zeros(out_ref.shape, jnp.float32)
    for i in range(grid):
        pooled = (sums[i] * (1.0 / (width * width))).astype(jnp.bfloat16)
        total = total + jnp.dot(
            pooled,
            proj_ref[i * lanes_out : (i + 1) * lanes_out],
            preferred_element_type=jnp.float32,
        )
    out_ref[...] = total.astype(out_ref.dtype)


def frame_rows(queries, padded, tables, proj, side, grid):
    count = queries.shape[0]

    def kernel(*refs):
        rows_kernel(side, grid, *refs)

    return pl.pallas_call(
        kernel,
        out_shape=jax.ShapeDtypeStruct((count, proj.shape[1]), jnp.bfloat16),
        in_specs=[VMEM] * 6,
        out_specs=VMEM,
        scratch_shapes=[
            pltpu.VMEM((side // 2, count, 4 * side), jnp.bfloat16),
            pltpu.VMEM((grid, count, proj.shape[0] // grid), jnp.float32),
        ],
        compiler_params=pltpu.CompilerParams(vmem_limit_bytes=32 * MIB),
        name="frame_rows",
    )(queries, padded, *tables, proj)


def layer_norm(values):
    center = values - jnp.mean(values, axis=-1, keepdims=True)
    spread = jnp.mean(center * center, axis=-1, keepdims=True)
    return center * lax.rsqrt(spread + 1e-05)


def mixer_kernel(
    tracks, rows_ref, place_ref, gain_ref, time_ref, up_hbm, down_hbm, out_ref, up_ref, down_ref, sems
):
    blocks, width, hidden_size = up_hbm.shape
    chunk = min(512, hidden_size)
    starts = range(0, hidden_size, chunk)
    ups, downs = {}, {}
    for block in range(blocks):
        for n, c in enumerate(starts):
            at = (block, slice(None), pl.ds(c, chunk))
            ups[block, n] = pltpu.make_async_copy(
                up_hbm.at[at], up_ref.at[at], sems.at[0, block, n]
            )
            ups[block, n].start()
        for n, c in enumerate(starts):
            at = (block, pl.ds(c, chunk))
            downs[block, n] = pltpu.make_async_copy(
                down_hbm.at[at], down_ref.at[at], sems.at[1, block, n]
            )
            downs[block, n].start()
    length = rows_ref.shape[0]
    slots = iota((length, length), 0)
    order = (slots == place_ref[...]).astype(jnp.bfloat16)
    state = jnp.dot(order, rows_ref[...], preferred_element_type=jnp.float32)
    edge = jnp.zeros((tracks, width), jnp.float32)
    for block in range(blocks):
        normed = layer_norm(state) * gain_ref[block, 0:1]
        before = jnp.concatenate([edge, normed[:-tracks]], axis=0)
        after = jnp.concatenate([normed[tracks:], edge], axis=0)
        state = (
            state
            + time_ref[block, 0:1] * before
            + time_ref[block, 1:2] * normed
            + time_ref[block, 2:3] * after
        )
        inner = (layer_norm(state) * gain_ref[block, 1:2]).astype(jnp.bfloat16)
        parts = []
        for n, c in enumerate(starts):
            ups[block, n].wait()
            hidden = jnp.dot(
                inner, up_ref[block, :, c : c + chunk], preferred_element_type=jnp.float32
            )
            parts.append(jax.nn.gelu(hidden, approximate=True).astype(jnp.bfloat16))
        for n, hidden in enumerate(parts):
            downs[block, n].wait()
            state = state + jnp.dot(
                hidden,
                down_ref[block, n * chunk : (n + 1) * chunk, :],
                preferred_element_type=jnp.float32,
            )
    out_ref[...] = lax.dot_general(
        order, state.astype(jnp.bfloat16), TN, preferred_element_type=jnp.float32
    ).astype(out_ref.dtype)


def mix_tracks(rows, place, norm_gains, time_kernels, mix_up, mix_down, tracks):
    def kernel(*refs):
        mixer_kernel(tracks, *refs)

    return pl.pallas_call(
        kernel,
        out_shape=jax.ShapeDtypeStruct(rows.shape, rows.dtype),
        in_specs=[VMEM] * 4 + [HBM, HBM],
        out_specs=VMEM,
        scratch_shapes=[
            pltpu.VMEM(mix_up.shape, mix_up.dtype),
            pltpu.VMEM(mix_down.shape, mix_down.dtype),
            pltpu.SemaphoreType.DMA((2, mix_up.shape[0], pl.cdiv(mix_up.shape[2], 512))),
        ],
        compiler_params=pltpu.CompilerParams(vmem_limit_bytes=53 * MIB),
        name="mixer",
    )(rows, place, norm_gains, time_kernels, mix_up, mix_down)


def on_device(
    features,
    query_frame,
    query_pos,
    frame_order,
    conv1_weight,
    conv1_bias,
    conv2_weight,
    proj_weight,
    norm_gains,
    time_kernels,
    mix_up,
    mix_down,
):
    devices = lax.axis_size(AXIS)
    tracks = query_frame.shape[0] // devices
    side = math.isqrt(features.shape[1])
    grid = math.isqrt(proj_weight.shape[0] // conv2_weight.shape[0])

    def make_tables(args):
        maps, *weights = args
        padded = jnp.pad(maps[0], ((side, side), (0, 0)))
        return padded, conv_tables(*weights, side, grid)

    def order_proj(weight):
        parts = weight.reshape(conv2_weight.shape[0], grid, grid, -1)
        return parts.transpose(1, 0, 2, 3).reshape(weight.shape)

    queries = pick_queries(features, query_frame, query_pos)
    work = (features, conv1_weight, conv1_bias, conv2_weight)
    if devices & (devices - 1):
        queries = lax.psum(queries, AXIS)
        padded, tables = make_tables(work)
        proj = order_proj(proj_weight)
    else:
        stages = exchange_stages(devices)
        queries = exchange(queries, stages[0], devices)
        queries, work = lax.optimization_barrier((queries, work))
        made = make_tables(work)
        queries = exchange(queries, stages[1], devices)
        queries, (padded, tables), proj_weight = lax.optimization_barrier(
            (queries, made, proj_weight)
        )
        proj = order_proj(proj_weight)
        for shifts in stages[2:]:
            queries = exchange(queries, shifts, devices)
    rows = frame_rows(queries, padded, tables, proj, side, grid)
    rows = lax.all_to_all(rows, AXIS, split_axis=0, concat_axis=0, tiled=True)
    place = (frame_order[:, None] * tracks + jnp.arange(tracks, dtype=jnp.int32)).reshape(1, -1)
    mixed = mix_tracks(rows, place, norm_gains, time_kernels, mix_up, mix_down, tracks)
    mixed = lax.all_to_all(mixed, AXIS, split_axis=0, concat_axis=0, tiled=True)
    return mixed[None]


def solution(mesh):
    placed = (
        P(("groups", "frames"), None, None),
        P("groups"),
        P("groups"),
        P("groups"),
        P(),
        P(),
        P(),
        P(),
        P(),
        P(),
        P(),
        P(),
    )
    return jax.shard_map(
        on_device,
        mesh=mesh,
        in_specs=placed,
        out_specs=P(("groups", "frames"), None, None),
        check_vma=False,
    )
```

time: 75.4 us -> 61.4 us (0.81)
  local copies, waits for them, and re-layouts: 15.5 us -> 1.92 us
  other arithmetic: 4.7 us -> 0.95 us
  Pallas kernels: 17.2 us -> 19.8 us
  starting transfers between devices: 11.7 us -> 13.3 us
  waiting for transfers between devices: 15.7 us -> 14.9 us
    unnamed x17, local copies, waits for them, and re-layouts: 5.98 us -> 0.05 us
    pallas_call x0 -> x2, Pallas kernels: none -> 4.28 us  [the longest x1 2.15 us: conv_tables(): pl.pallas_call(kernel, out_shape=[jax.ShapeDtypeStruct((4 * side, side //...]
    pallas_call x1, Pallas kernels: 13.5 us -> 10.2 us  [frame_rows(): pl.pallas_call(kernel, out_shape=jax.ShapeDtypeStruct((count, proj.shape[...]
    reshape x2 -> x1, local copies, waits for them, and re-layouts: 2.86 us -> 0.17 us  [order_proj(): parts = weight.reshape(conv2_weight.shape[0], grid, grid, -1)]
    broadcast_in_dim x19 -> x0, local copies, waits for them, and re-layouts: 2.54 us -> none  [the longest x18 2.47 us: conv_tables(): jnp.broadcast_to(taps[:, None, :, None], (9, width * grid, ch1, 4))]
    gather x1 -> x0, local copies, waits for them, and re-layouts: 1.99 us -> none  [on_device(): features[0, query_pos]]
    pallas_call x1, Pallas kernels: 3.67 us -> 5.31 us  [mix_tracks(): pl.pallas_call(kernel, out_shape=jax.ShapeDtypeStruct(rows.shape, rows.dt...]
    select_n x2 -> x0, other arithmetic: 1.49 us -> none  [the longest x1 1.4 us: conv_tables(): jnp.where(diff == dy * (4 * side) + dx, taps[3 * dy + dx][None, :], first)]
  transfers between devices with their start and end apart: 8 -> 8, of which waited for: 6 -> 6; matrix products, arithmetic and copies ran while one was open for 11% -> 1% of each run, Pallas kernels for 0% -> 4%
where the time goes in v2:
time: 61.4 us; the launch traced here: 61.1 us
  Pallas kernels  19.8 us (32%)
  waiting for transfers between devices  14.9 us (24%)
  starting transfers between devices  13.3 us (22%)
  blocking collectives  10 us (16%)
  local copies, waits for them, and re-layouts  1.92 us (3%)
  other arithmetic  0.95 us (2%)
    pallas_call x1, Pallas kernels, frame_rows(): pl.pallas_call(kernel, out_shape=jax.ShapeDtypeStruct((count, proj.shape[...  10.2 us
    all_to_all x1, blocking collectives, on_device(): mixed = lax.all_to_all(mixed, AXIS, split_axis=0, concat_axis=0, tiled=True)  10 us
    ppermute x7, starting transfers between devices, exchange(): lax.ppermute(values, AXIS, [(i, i ^ shift) for i in range(devices)])  9.47 us
    all_to_all x1, waiting for transfers between devices, on_device(): rows = lax.all_to_all(rows, AXIS, split_axis=0, concat_axis=0, tiled=True)  8 us
    ppermute x7, waiting for transfers between devices, exchange(): lax.ppermute(values, AXIS, [(i, i ^ shift) for i in range(devices)])  6.89 us
    pallas_call x1, Pallas kernels, mix_tracks(): pl.pallas_call(kernel, out_shape=jax.ShapeDtypeStruct(rows.shape, rows.dt...  5.31 us
    all_to_all x1, starting transfers between devices, on_device(): rows = lax.all_to_all(rows, AXIS, split_axis=0, concat_axis=0, tiled=True)  3.84 us
    pallas_call x1, Pallas kernels, conv_tables(): pl.pallas_call(kernel, out_shape=[jax.ShapeDtypeStruct((4 * side, side //...  2.15 us
  transfers between devices with their start and end apart: 8, of which 6 were waited for; matrix products, arithmetic and copies ran while one was open for 1% of the time, Pallas kernels for 4%

profile of v2, /device:TPU:0, one launch (start us, length us, event | category | flops | bytes accessed | tf_op | source)
XLA Modules:
  0.0 61.1 jit_solution(4701291718041886548)
XLA Ops:
  0.0 0.0 copy-start.4
  0.0 0.8 %fusion.refs_0_ = s32[1,128]{1,0:T(1,128)S(1)} fusion(s32[128]{0:T(128)} %param.14, s32[128]{0:T(128)} %param.13, s32[]{:T(128)S(6)} %axis_index.12), kind=kLoop, calls=%fused_computation.4 | loop fusion | flops 256 | bytes 1540 | tf_op jit(solution)/shard_map/reshape | solution.py:89
  0.8 2.1 %pick_queries.1 = bf16[128,256]{1,0:T(8,128)(2,1)S(1)} custom-call(s32[1,128]{1,0:T(1,128)S(1)} %fusion.refs_0_, bf16[1,4096,256]{2,1,0:T(8,128)(2,1)} %refs_1_.1), custom_call_target="tpu_custom_call" | custom-call | tf_op jit(solution)/shard_map/pick_queries/pallas_call | solution.py:78
  3.0 0.5 collective-permute-start
  3.5 0.9 %collective-permute-done = bf16[128,256]{1,0:T(8,128)(2,1)S(1)} collective-permute-done((bf16[128,256]{1,0:T(8,128)(2,1)S(1)}, bf16[128,256]{1,0:T(8,128)(2,1)S(1)}, u32[]{:S(2)}, u32[]{:S(2)}) %collective-permute-start) | collective-permute-done | bytes 65568 | tf_op jit(solution)/shard_map/ppermute | solution.py:36
  4.4 0.0 copy-start
  4.4 0.0 copy-start.2
  4.4 0.0 copy-start.3
  4.5 3.9 %collective-permute-start.3 = (bf16[128,256]{1,0:T(8,128)(2,1)S(1)}, bf16[128,256]{1,0:T(8,128)(2,1)S(1)}, u32[]{:S(2)}, u32[]{:S(2)}) collective-permute-start(bf16[128,256]{1,0:T(8,128)(2,1)S(1)} %add.46), channel_id=1, source_target_pairs={{0,6},{1,7},{2,4},{3,5},{4,2},{5,3},{6,0},{7,1},{8,14},{9,15},{10,... | collective-permute-start | bytes 196616 | tf_op jit(solution)/shard_map/ppermute | solution.py:36
  8.3 0.5 collective-permute-start.2
  8.8 0.1 collective-permute-start.1
  9.0 0.0 copy-done.4
  9.0 0.0 copy-start.5
  9.0 0.1 pad.4.refs_1_
  9.1 0.0 copy-done
  9.1 0.0 copy-done.2
  9.1 0.0 copy-done.3
  9.1 2.1 %conv_tables.1 = (bf16[256,2048]{1,0:T(8,128)(2,1)S(1)}, f32[1,512]{1,0:T(1,128)S(1)}, bf16[512,256]{1,0:T(8,128)(2,1)S(1)}) custom-call(f32[16,9]{1,0:T(8,128)S(1)} %copy-done.2, f32[1,16]{1,0:T(1,128)S(1)} %bitcast.13, bf16[64,32]{1,0:T(8,128)(2,1)S(1)} %bitcast.12), custom_call_target="tpu_custom_call" | custom-call | tf_op jit(solution)/shard_map/conv_tables/pallas_call | solution.py:138
  11.3 0.0 collective-permute-done.3
  11.3 1.3 %collective-permute-done.2 = bf16[128,256]{1,0:T(8,128)(2,1)S(1)} collective-permute-done((bf16[128,256]{1,0:T(8,128)(2,1)S(1)}, bf16[128,256]{1,0:T(8,128)(2,1)S(1)}, u32[]{:S(2)}, u32[]{:S(2)}) %collective-permute-start.2) | collective-permute-done | bytes 65568 | tf_op jit(solution)/shard_map/ppermute | solution.py:36
  12.6 0.5 collective-permute-done.1
  13.1 3.7 %collective-permute-start.6 = (bf16[128,256]{1,0:T(8,128)(2,1)S(1)}, bf16[128,256]{1,0:T(8,128)(2,1)S(1)}, u32[]{:S(2)}, u32[]{:S(2)}) collective-permute-start(bf16[128,256]{1,0:T(8,128)(2,1)S(1)} %add_add_fusion.1), channel_id=1, source_target_pairs={{0,24},{1,25},{2,26},{3,27},{4,28},{5,29},{6,30},{7,31},{8,16},{9,... | collective-permute-start | bytes 196616 | tf_op jit(solution)/shard_map/ppermute | solution.py:36
  16.8 0.0 collective-permute-start.5
  16.8 0.8 %collective-permute-start.4 = (bf16[128,256]{1,0:T(8,128)(2,1)S(1)}, bf16[128,256]{1,0:T(8,128)(2,1)S(1)}, u32[]{:S(2)}, u32[]{:S(2)}) collective-permute-start(bf16[128,256]{1,0:T(8,128)(2,1)S(1)} %add_add_fusion.1), channel_id=1, source_target_pairs={{0,8},{1,9},{2,10},{3,11},{4,12},{5,13},{6,14},{7,15},{8,0},{9,1},... | collective-permute-start | bytes 196616 | tf_op jit(solution)/shard_map/ppermute | solution.py:36
  17.6 0.0 copy-done.5
  17.6 0.2 copy.15
  17.7 1.5 %collective-permute-done.6 = bf16[128,256]{1,0:T(8,128)(2,1)S(1)} collective-permute-done((bf16[128,256]{1,0:T(8,128)(2,1)S(1)}, bf16[128,256]{1,0:T(8,128)(2,1)S(1)}, u32[]{:S(2)}, u32[]{:S(2)}) %collective-permute-start.6) | collective-permute-done | bytes 65568 | tf_op jit(solution)/shard_map/ppermute | solution.py:36
  19.2 2.7 %collective-permute-done.5 = bf16[128,256]{1,0:T(8,128)(2,1)S(1)} collective-permute-done((bf16[128,256]{1,0:T(8,128)(2,1)S(1)}, bf16[128,256]{1,0:T(8,128)(2,1)S(1)}, u32[]{:S(2)}, u32[]{:S(2)}) %collective-permute-start.5) | collective-permute-done | bytes 65568 | tf_op jit(solution)/shard_map/ppermute | solution.py:36
  21.9 0.0 collective-permute-done.4
  22.0 0.0 copy-start.7
  22.0 0.0 copy-start.6
  22.0 0.0 copy-start.1
  22.0 10.2 %frame_rows.1 = bf16[128,512]{1,0:T(8,128)(2,1)S(1)} custom-call(bf16[128,256]{1,0:T(8,128)(2,1)S(1)} %add_add_fusion.refs_0_, bf16[4224,256]{1,0:T(8,128)(2,1)S(1)} %pad.4.refs_1_, bf16[256,2048]{1,0:T(8,128)(2,1)S(1)} %get-tuple-element.29.refs_2_, f32[1,512]{1,0:T(1,128)S(1)} %get-tuple-element.30.refs_3_, ...), custom_call_target="tpu_custom_call" | custom-call | tf_op jit(solution)/shard_map/frame_rows/pallas_call | solution.py:204
  32.2 0.7 %all_to_all.13 = bf16[32,4,512]{2,1,0:T(4,128)(2,1)} reshape(bf16[128,512]{1,0:T(8,128)(2,1)S(1)} %frame_rows.1) | data formatting | bytes 262144 | tf_op jit(solution)/shard_map/all_to_all | solution.py:345
  32.9 3.8 %all-to-all-start = ((bf16[32,4,512]{2,1,0:T(4,128)(2,1)}), bf16[32,4,512]{2,1,0:T(4,128)(2,1)S(1)}, u32[]{:S(2)}, u32[]{:S(2)}) async-start(bf16[32,4,512]{2,1,0:T(4,128)(2,1)} %all_to_all.13), calls=%async_computation | async-start | bytes 262144 | tf_op jit(solution)/shard_map/all_to_all | solution.py:345
  36.8 0.0 copy-done.7
  36.8 0.1 iota_add_fusion
  36.9 0.1 add.56.refs_1_
  37.0 0.0 copy-done.6
  37.0 8.0 %all-to-all-done = bf16[32,4,512]{2,1,0:T(4,128)(2,1)S(1)} async-done(((bf16[32,4,512]{2,1,0:T(4,128)(2,1)}), bf16[32,4,512]{2,1,0:T(4,128)(2,1)S(1)}, u32[]{:S(2)}, u32[]{:S(2)}) %all-to-all-start) | async-done | bytes 131104 | tf_op jit(solution)/shard_map/all_to_all | solution.py:345
  45.1 0.0 copy-done.1
  45.1 5.3 %mixer.1 = bf16[128,512]{1,0:T(8,128)(2,1)S(1)} custom-call(bf16[128,512]{1,0:T(8,128)(2,1)S(1)} %all_to_all.15.refs_0_, s32[1,128]{1,0:T(1,128)S(1)} %add.56.refs_1_, f32[2,2,512]{2,1,0:T(2,128)S(1)} %copy-done.1, f32[2,3,512]{2,1,0:T(4,128)S(1)} %copy.16.refs_3_, bf16[2,512,2048]{2,1,0:T(8,128)(2,1)} %refs_4_.1, bf16[2,2048,512]{2,1,0:T(8,128)(2,1)} %refs_5_.1), custom_call_target="tpu_custom_call" | custom-call | tf_op jit(solution)/shard_map/mixer/pallas_call | solution.py:283
  50.4 10.0 %all_to_all.20 = bf16[32,4,512]{2,1,0:T(4,128)(2,1)S(1)} all-to-all(bf16[32,4,512]{2,1,0:T(4,128)(2,1)S(1)} %all_to_all.16), channel_id=1, replica_groups=mesh['groups'=1,'frames'=32] {'frames'}, dimensions={0} | all-to-all | bytes 262144 | tf_op jit(solution)/shard_map/all_to_all | solution.py:348
  60.4 0.7 %broadcast_in_dim.10 = bf16[1,128,512]{2,1,0:T(8,128)(2,1)} reshape(bf16[32,4,512]{2,1,0:T(4,128)(2,1)S(1)} %all_to_all.20) | data formatting | bytes 262144 | tf_op jit(solution)/shard_map/broadcast_in_dim | solution.py:349
  (7 shorter events, 0.1 us)
Async XLA Ops:
  0.0 9.0 %copy-start.4 = (bf16[1,4096,256]{2,1,0:T(8,128)(2,1)S(1)}, bf16[1,4096,256]{2,1,0:T(8,128)(2,1)}, u32[]{:S(2)}) copy-start(bf16[1,4096,256]{2,1,0:T(8,128)(2,1)} %refs_1_.1) | copy-start | bytes 6291460
  3.0 1.4 %collective-permute-start = (bf16[128,256]{1,0:T(8,128)(2,1)S(1)}, bf16[128,256]{1,0:T(8,128)(2,1)S(1)}, u32[]{:S(2)}, u32[]{:S(2)}) collective-permute-start(bf16[128,256]{1,0:T(8,128)(2,1)S(1)} %pick_queries.1), channel_id=1, source_target_pairs={{0,1},{1,0},{2,3},{3,2},{4,5},{5,4},{6,7},{7,6},{8,9},{9,8},{10,11... | collective-permute-start | bytes 196616 | tf_op jit(solution)/shard_map/ppermute | solution.py:36
  4.4 4.7 %copy-start = (bf16[32,16,2,2]{0,3,2,1:T(2,128)(2,1)S(1)}, bf16[32,16,2,2]{0,3,2,1:T(2,128)(2,1)}, u32[]{:S(2)}) copy-start(bf16[32,16,2,2]{0,3,2,1:T(2,128)(2,1)} %param.18) | copy-start | bytes 12292
  4.4 4.7 %copy-start.2 = (f32[16,9]{1,0:T(8,128)S(1)}, f32[16,9]{1,0:T(8,128)}, u32[]{:S(2)}) copy-start(f32[16,9]{1,0:T(8,128)} %refs_0_) | copy-start | bytes 1732
  4.4 4.7 %copy-start.3 = (f32[16]{0:T(128)S(1)}, f32[16]{0:T(128)}, u32[]{:S(2)}) copy-start(f32[16]{0:T(128)} %param.17) | copy-start | bytes 196
  4.5 6.8 %collective-permute-start.3 = (bf16[128,256]{1,0:T(8,128)(2,1)S(1)}, bf16[128,256]{1,0:T(8,128)(2,1)S(1)}, u32[]{:S(2)}, u32[]{:S(2)}) collective-permute-start(bf16[128,256]{1,0:T(8,128)(2,1)S(1)} %add.46), channel_id=1, source_target_pairs={{0,6},{1,7},{2,4},{3,5},{4,2},{5,3},{6,0},{7,1},{8,14},{9,15},{10,... | collective-permute-start | bytes 196616 | tf_op jit(solution)/shard_map/ppermute | solution.py:36
  8.3 4.3 %collective-permute-start.2 = (bf16[128,256]{1,0:T(8,128)(2,1)S(1)}, bf16[128,256]{1,0:T(8,128)(2,1)S(1)}, u32[]{:S(2)}, u32[]{:S(2)}) collective-permute-start(bf16[128,256]{1,0:T(8,128)(2,1)S(1)} %add.46), channel_id=1, source_target_pairs={{0,4},{1,5},{2,6},{3,7},{4,0},{5,1},{6,2},{7,3},{8,12},{9,13},{10,... | collective-permute-start | bytes 196616 | tf_op jit(solution)/shard_map/ppermute | solution.py:36
  8.8 4.3 %collective-permute-start.1 = (bf16[128,256]{1,0:T(8,128)(2,1)S(1)}, bf16[128,256]{1,0:T(8,128)(2,1)S(1)}, u32[]{:S(2)}, u32[]{:S(2)}) collective-permute-start(bf16[128,256]{1,0:T(8,128)(2,1)S(1)} %add.46), channel_id=1, source_target_pairs={{0,2},{1,3},{2,0},{3,1},{4,6},{5,7},{6,4},{7,5},{8,10},{9,11},{10,... | collective-permute-start | bytes 196616 | tf_op jit(solution)/shard_map/ppermute | solution.py:36
  9.0 8.6 %copy-start.5 = (bf16[2048,512]{1,0:T(8,128)(2,1)S(1)}, bf16[2048,512]{1,0:T(8,128)(2,1)}, u32[]{:S(2)}) copy-start(bf16[2048,512]{1,0:T(8,128)(2,1)} %param.19) | copy-start | bytes 6291460
  13.1 6.1 %collective-permute-start.6 = (bf16[128,256]{1,0:T(8,128)(2,1)S(1)}, bf16[128,256]{1,0:T(8,128)(2,1)S(1)}, u32[]{:S(2)}, u32[]{:S(2)}) collective-permute-start(bf16[128,256]{1,0:T(8,128)(2,1)S(1)} %add_add_fusion.1), channel_id=1, source_target_pairs={{0,24},{1,25},{2,26},{3,27},{4,28},{5,29},{6,30},{7,31},{8,16},{9,... | collective-permute-start | bytes 196616 | tf_op jit(solution)/shard_map/ppermute | solution.py:36
  16.8 5.2 %collective-permute-start.5 = (bf16[128,256]{1,0:T(8,128)(2,1)S(1)}, bf16[128,256]{1,0:T(8,128)(2,1)S(1)}, u32[]{:S(2)}, u32[]{:S(2)}) collective-permute-start(bf16[128,256]{1,0:T(8,128)(2,1)S(1)} %add_add_fusion.1), channel_id=1, source_target_pairs={{0,16},{1,17},{2,18},{3,19},{4,20},{5,21},{6,22},{7,23},{8,24},{9,... | collective-permute-start | bytes 196616 | tf_op jit(solution)/shard_map/ppermute | solution.py:36
  16.8 5.2 %collective-permute-start.4 = (bf16[128,256]{1,0:T(8,128)(2,1)S(1)}, bf16[128,256]{1,0:T(8,128)(2,1)S(1)}, u32[]{:S(2)}, u32[]{:S(2)}) collective-permute-start(bf16[128,256]{1,0:T(8,128)(2,1)S(1)} %add_add_fusion.1), channel_id=1, source_target_pairs={{0,8},{1,9},{2,10},{3,11},{4,12},{5,13},{6,14},{7,15},{8,0},{9,1},... | collective-permute-start | bytes 196616 | tf_op jit(solution)/shard_map/ppermute | solution.py:36
  22.0 14.8 %copy-start.7 = (s32[32]{0:T(128)S(1)}, s32[32]{0:T(128)}, u32[]{:S(2)}) copy-start(s32[32]{0:T(128)} %param.15) | copy-start | bytes 388
  22.0 15.0 %copy-start.6 = (f32[2,3,512]{2,0,1:T(2,128)S(1)}, f32[2,3,512]{2,0,1:T(2,128)}, u32[]{:S(2)}) copy-start(f32[2,3,512]{2,0,1:T(2,128)} %param.21) | copy-start | bytes 36868
  22.0 23.1 %copy-start.1 = (f32[2,2,512]{2,1,0:T(2,128)S(1)}, f32[2,2,512]{2,1,0:T(2,128)}, u32[]{:S(2)}) copy-start(f32[2,2,512]{2,1,0:T(2,128)} %refs_2_.1) | copy-start | bytes 24580
  32.9 12.1 %all-to-all-start = ((bf16[32,4,512]{2,1,0:T(4,128)(2,1)}), bf16[32,4,512]{2,1,0:T(4,128)(2,1)S(1)}, u32[]{:S(2)}, u32[]{:S(2)}) async-start(bf16[32,4,512]{2,1,0:T(4,128)(2,1)} %all_to_all.13), calls=%async_computation | async-start | bytes 262144 | tf_op jit(solution)/shard_map/all_to_all | solution.py:345

commit v3 on v2

--- a/solution.py
+++ b/solution.py
@@ -96,41 +96,47 @@
     width = side // 2 // grid
     lanes = grid * ch1 * 4
     rows = 4 * side
-    lane = iota((1, lanes), 1)
-    hot = (iota((ch1, lanes), 0) == iota((ch1, lanes), 1) // 4 % ch1).astype(jnp.float32)
+    hot = (iota((lanes, ch1), 1) == iota((lanes, ch1), 0) // 4 % ch1).astype(jnp.float32)
     lane_bias_ref[...] = jnp.dot(
-        bias_ref[...], hot, precision=lax.Precision.HIGHEST, preferred_element_type=jnp.float32
-    )
-    taps = lax.dot_general(
-        taps_ref[...].astype(jnp.bfloat16),
-        hot.astype(jnp.bfloat16),
-        TN,
+        hot * bias_ref[...],
+        jnp.ones((ch1, lane_bias_ref.shape[1]), jnp.float32),
+        precision=lax.Precision.HIGHEST,
         preferred_element_type=jnp.float32,
     )
-    at = lane // 2 % 2 * rows + 2 * width * (lane // (4 * ch1)) + lane % 2 - 1
-    spot = iota((rows, 1), 0)
+    hot = hot.astype(jnp.bfloat16)
+    taps = [
+        jnp.dot(
+            hot,
+            jnp.broadcast_to(taps_ref[:, n : n + 1], (ch1, rows)).astype(jnp.bfloat16),
+            preferred_element_type=jnp.float32,
+        )
+        for n in range(9)
+    ]
+    row = iota((lanes, 1), 0)
+    at = row // 2 % 2 * rows + 2 * width * (row // (4 * ch1)) + row % 2 - 1
+    spot = iota((1, rows), 1)
     diff = spot // side * rows + spot % side - at
     for s in range(width):
-        first = jnp.zeros((rows, lanes), jnp.float32)
+        first = jnp.zeros((lanes, rows), jnp.float32)
         for dy in range(3):
             for dx in range(3):
-                n = 3 * dy + dx
-                first = jnp.where(diff == dy * rows + dx + 2 * s, taps[n : n + 1], first)
-        first_ref[:, s * lanes : (s + 1) * lanes] = first.astype(jnp.bfloat16)
-
-    out_lanes = ch2 * grid
-    hot = (iota((ch2, out_lanes), 0) == iota((ch2, out_lanes), 1) // grid).astype(jnp.bfloat16)
-    wide = jnp.dot(small_ref[...], hot, preferred_element_type=jnp.float32)
-    for j in range(grid):
-        second_ref[j * 4 * ch1 : (j + 1) * 4 * ch1] = jnp.where(
-            iota(wide.shape, 1) % grid == j, wide, 0.0
-        ).astype(jnp.bfloat16)
+                first = jnp.where(diff == dy * rows + dx + 2 * s, taps[3 * dy + dx], first)
+        first_ref[s * lanes : (s + 1) * lanes] = first.astype(jnp.bfloat16)
+
+    outs, ins = second_ref.shape
+    group = outs // ch2
+    hot = (iota((outs, ch2), 1) == iota((outs, ch2), 0) // group).astype(jnp.bfloat16)
+    small = jnp.concatenate([small_ref[...]] * group, axis=0)
+    wide = lax.dot_general(hot, small, NT, preferred_element_type=jnp.float32)
+    same = iota((outs, ins), 0) % group == iota((outs, ins), 1) // (4 * ch1)
+    second_ref[...] = jnp.where(same, wide, 0.0).astype(jnp.bfloat16)
 
 
 def conv_tables(conv1_weight, conv1_bias, conv2_weight, side, grid):
     ch1 = conv1_weight.shape[0]
     ch2 = conv2_weight.shape[0]
     lanes = grid * ch1 * 4
+    group = grid // column_groups(grid, ch1)
 
     def kernel(*refs):
         tables_kernel(side, grid, *refs)
@@ -138,9 +144,9 @@
     return pl.pallas_call(
         kernel,
         out_shape=[
-            jax.ShapeDtypeStruct((4 * side, side // 2 // grid * lanes), jnp.bfloat16),
-            jax.ShapeDtypeStruct((1, lanes), jnp.float32),
-            jax.ShapeDtypeStruct((lanes, ch2 * grid), jnp.bfloat16),
+            jax.ShapeDtypeStruct((side // 2 // grid * lanes, 4 * side), jnp.bfloat16),
+            jax.ShapeDtypeStruct((lanes, 128), jnp.float32),
+            jax.ShapeDtypeStruct((group * ch2, group * ch1 * 4), jnp.bfloat16),
         ],
         in_specs=[VMEM] * 3,
         out_specs=[VMEM] * 3,
@@ -149,53 +155,113 @@
     )(conv1_weight, conv1_bias.reshape(1, ch1), conv2_weight.transpose(1, 2, 3, 0).reshape(ch1 * 4, ch2))
 
 
+def column_groups(grid, ch1):
+    return max(1, grid * ch1 * 4 // 256)
+
+
+def proj_kernel(groups, size, proj_ref, out_ref):
+    grid_columns = size
+    total, columns = proj_ref.shape
+    block = total // grid_columns
+    group = grid_columns // groups
+    to = iota((block, block), 0)
+    per = block // groups
+    source = to % per // group * grid_columns + to // per * group + to % group
+    move = (iota((block, block), 1) == source).astype(jnp.bfloat16)
+    for i in range(total // block):
+        at = pl.ds(i * block, block)
+        out_ref[at] = jnp.dot(
+            move, proj_ref[at], preferred_element_type=jnp.float32
+        ).astype(out_ref.dtype)
+
+
+def order_proj(weight, ch1, ch2, grid):
+    parts = weight.reshape(ch2, grid, grid, -1).transpose(1, 0, 2, 3).reshape(weight.shape)
+
+    def kernel(*refs):
+        proj_kernel(column_groups(grid, ch1), grid, *refs)
+
+    return pl.pallas_call(
+        kernel,
+        out_shape=jax.ShapeDtypeStruct(weight.shape, weight.dtype),
+        in_specs=[VMEM],
+        out_specs=VMEM,
+        compiler_params=pltpu.CompilerParams(vmem_limit_bytes=16 * MIB),
+        name="order_proj",
+    )(parts)
+
+
 def rows_kernel(
-    side, grid, query_ref, feat_ref, first_ref, bias_ref, second_ref, proj_ref, out_ref, windows, sums
+    side, grid, query_ref, feat_ref, first_ref, bias_ref, second_ref, proj_ref, out_ref,
+    corr, hold,
 ):
     half = side // 2
     width = half // grid
     count, channels = query_ref.shape
-    query = query_ref[...]
+    points = feat_ref.shape[1]
     scale = 1.0 / math.sqrt(channels)
     step = 2 * side
-    for t in range(half + 1):
+    edge = jnp.zeros((side, count), corr.dtype)
+    corr[pl.ds(0, side)] = edge
+    corr[pl.ds(side + points, side)] = edge
+    query = query_ref[...]
+    piece = min(512, points)
+    for at in range(0, points, piece):
         part = lax.dot_general(
-            query, feat_ref[t * step : (t + 1) * step], NT, preferred_element_type=jnp.float32
-        )
-        part = (part * scale).astype(jnp.bfloat16)
-        if t < half:
-            windows[t, :, :step] = part
-        if t > 0:
-            windows[t - 1, :, step:] = part
+            feat_ref[0, at : at + piece], query, NT, preferred_element_type=jnp.float32
+        )
+        corr[side + at : side + at + piece] = (part * scale).astype(corr.dtype)
     bias = bias_ref[...]
-    lanes_in, lanes_out = second_ref.shape
-    for s in range(width):
-        for i in range(grid):
-            window = windows[i * width : (i + 1) * width].reshape(width * count, 2 * step)
+    bias = jnp.concatenate([bias] * (2 * count // bias.shape[1]), axis=1)
+    second = second_ref[...]
+    lanes = bias.shape[0]
+    outs, ins = second.shape
+    groups = lanes // ins
+    slots = hold.shape[0]
+    sums = {}
+
+    def strided(step_number, i):
+        for g in range(groups):
+            two = jnp.dot(
+                second,
+                hold[step_number % slots, g * ins : (g + 1) * ins],
+                preferred_element_type=jnp.float32,
+            )
+            two = jnp.maximum(two, 0.0)
+            two = two[:, :count] + two[:, count:]
+            sums[i, g] = sums[i, g] + two if (i, g) in sums else two
+
+    waiting = []
+    for y in range(0, half, 2):
+        window = jnp.concatenate([corr[n * step : (n + 2) * step] for n in (y, y + 1)], axis=1)
+        for s in range(width):
             one = jnp.dot(
+                first_ref[s * lanes : (s + 1) * lanes],
                 window,
-                first_ref[:, s * lanes_in : (s + 1) * lanes_in],
                 preferred_element_type=jnp.float32,
             )
-            one = jnp.maximum(one + bias, 0.0).astype(jnp.bfloat16)
-            two = jnp.dot(one, second_ref[...], preferred_element_type=jnp.float32)
-            two = jnp.maximum(two, 0.0).reshape(width, count, lanes_out)
-            summed = two[0]
-            for u in range(1, width):
-                summed = summed + two[u]
-            sums[i] = summed if s == 0 else sums[i] + summed
+            number = y // 2 * width + s
+            hold[number % slots] = jnp.maximum(one + bias, 0.0).astype(jnp.bfloat16)
+            waiting.append((number, y // width))
+            if len(waiting) > slots // 2:
+                strided(*waiting.pop(0))
+    for late in waiting:
+        strided(*late)
     total = jnp.zeros(out_ref.shape, jnp.float32)
+    block = groups * outs
     for i in range(grid):
-        pooled = (sums[i] * (1.0 / (width * width))).astype(jnp.bfloat16)
-        total = total + jnp.dot(
+        pooled = jnp.concatenate([sums[i, g] for g in range(groups)], axis=0)
+        pooled = (pooled * (1.0 / (width * width))).astype(jnp.bfloat16)
+        total = total + lax.dot_general(
             pooled,
-            proj_ref[i * lanes_out : (i + 1) * lanes_out],
+            proj_ref[i * block : (i + 1) * block],
+            TN,
             preferred_element_type=jnp.float32,
         )
     out_ref[...] = total.astype(out_ref.dtype)
 
 
-def frame_rows(queries, padded, tables, proj, side, grid):
+def frame_rows(queries, features, tables, proj, side, grid):
     count = queries.shape[0]
 
     def kernel(*refs):
@@ -207,12 +273,12 @@
         in_specs=[VMEM] * 6,
         out_specs=VMEM,
         scratch_shapes=[
-            pltpu.VMEM((side // 2, count, 4 * side), jnp.bfloat16),
-            pltpu.VMEM((grid, count, proj.shape[0] // grid), jnp.float32),
+            pltpu.VMEM((features.shape[1] + 2 * side, count), jnp.bfloat16),
+            pltpu.VMEM((8, tables[1].shape[0], 2 * count), jnp.bfloat16),
         ],
         compiler_params=pltpu.CompilerParams(vmem_limit_bytes=32 * MIB),
         name="frame_rows",
-    )(queries, padded, *tables, proj)
+    )(queries, features, *tables, proj)
 
 
 def layer_norm(values):
@@ -225,7 +291,7 @@
     tracks, rows_ref, place_ref, gain_ref, time_ref, up_hbm, down_hbm, out_ref, up_ref, down_ref, sems
 ):
     blocks, width, hidden_size = up_hbm.shape
-    chunk = min(512, hidden_size)
+    chunk = min(1024, hidden_size)
     starts = range(0, hidden_size, chunk)
     ups, downs = {}, {}
     for block in range(blocks):
@@ -242,8 +308,15 @@
             )
             downs[block, n].start()
     length = rows_ref.shape[0]
-    slots = iota((length, length), 0)
-    order = (slots == place_ref[...]).astype(jnp.bfloat16)
+    frames = place_ref.shape[1]
+    spread = (iota((frames, length), 0) == iota((frames, length), 1) // tracks).astype(jnp.float32)
+    time = jnp.dot(
+        jnp.broadcast_to(place_ref[...].astype(jnp.float32), (8, frames)),
+        spread,
+        preferred_element_type=jnp.float32,
+    )[0:1]
+    place = time.astype(jnp.int32) * tracks + iota((1, length), 1) % tracks
+    order = (iota((length, length), 0) == place).astype(jnp.bfloat16)
     state = jnp.dot(order, rows_ref[...], preferred_element_type=jnp.float32)
     edge = jnp.zeros((tracks, width), jnp.float32)
     for block in range(blocks):
@@ -252,9 +325,9 @@
         after = jnp.concatenate([normed[tracks:], edge], axis=0)
         state = (
             state
-            + time_ref[block, 0:1] * before
-            + time_ref[block, 1:2] * normed
-            + time_ref[block, 2:3] * after
+            + time_ref[0, block : block + 1] * before
+            + time_ref[1, block : block + 1] * normed
+            + time_ref[2, block : block + 1] * after
         )
         inner = (layer_norm(state) * gain_ref[block, 1:2]).astype(jnp.bfloat16)
         parts = []
@@ -288,7 +361,7 @@
         scratch_shapes=[
             pltpu.VMEM(mix_up.shape, mix_up.dtype),
             pltpu.VMEM(mix_down.shape, mix_down.dtype),
-            pltpu.SemaphoreType.DMA((2, mix_up.shape[0], pl.cdiv(mix_up.shape[2], 512))),
+            pltpu.SemaphoreType.DMA((2, mix_up.shape[0], pl.cdiv(mix_up.shape[2], 1024))),
         ],
         compiler_params=pltpu.CompilerParams(vmem_limit_bytes=53 * MIB),
         name="mixer",
@@ -314,37 +387,27 @@
     side = math.isqrt(features.shape[1])
     grid = math.isqrt(proj_weight.shape[0] // conv2_weight.shape[0])
 
-    def make_tables(args):
-        maps, *weights = args
-        padded = jnp.pad(maps[0], ((side, side), (0, 0)))
-        return padded, conv_tables(*weights, side, grid)
-
-    def order_proj(weight):
-        parts = weight.reshape(conv2_weight.shape[0], grid, grid, -1)
-        return parts.transpose(1, 0, 2, 3).reshape(weight.shape)
-
     queries = pick_queries(features, query_frame, query_pos)
-    work = (features, conv1_weight, conv1_bias, conv2_weight)
+    ch1, ch2 = conv1_weight.shape[0], conv2_weight.shape[0]
+    convs = (conv1_weight, conv1_bias, conv2_weight)
     if devices & (devices - 1):
         queries = lax.psum(queries, AXIS)
-        padded, tables = make_tables(work)
-        proj = order_proj(proj_weight)
+        tables = conv_tables(*convs, side, grid)
+        proj = order_proj(proj_weight, ch1, ch2, grid)
     else:
         stages = exchange_stages(devices)
         queries = exchange(queries, stages[0], devices)
-        queries, work = lax.optimization_barrier((queries, work))
-        made = make_tables(work)
+        queries, convs = lax.optimization_barrier((queries, convs))
+        tables = conv_tables(*convs, side, grid)
         queries = exchange(queries, stages[1], devices)
-        queries, (padded, tables), proj_weight = lax.optimization_barrier(
-            (queries, made, proj_weight)
-        )
-        proj = order_proj(proj_weight)
+        queries, tables, proj_weight = lax.optimization_barrier((queries, tables, proj_weight))
+        proj = order_proj(proj_weight, ch1, ch2, grid)
         for shifts in stages[2:]:
             queries = exchange(queries, shifts, devices)
-    rows = frame_rows(queries, padded, tables, proj, side, grid)
+    rows = frame_rows(queries, features, tables, proj, side, grid)
     rows = lax.all_to_all(rows, AXIS, split_axis=0, concat_axis=0, tiled=True)
-    place = (frame_order[:, None] * tracks + jnp.arange(tracks, dtype=jnp.int32)).reshape(1, -1)
-    mixed = mix_tracks(rows, place, norm_gains, time_kernels, mix_up, mix_down, tracks)
+    place = frame_order.reshape(1, -1)
+    mixed = mix_tracks(rows, place, norm_gains, time_kernels.transpose(1, 0, 2), mix_up, mix_down, tracks)
     mixed = lax.all_to_all(mixed, AXIS, split_axis=0, concat_axis=0, tiled=True)
     return mixed[None]
 

time: 61.4 us -> 56.9 us (0.927)
  blocking collectives: 10 us -> 21.9 us
  waiting for transfers between devices: 14.9 us -> 6.62 us
  starting transfers between devices: 13.3 us -> 9.49 us
  Pallas kernels: 19.8 us -> 16.7 us
  local copies, waits for them, and re-layouts: 1.92 us -> 1.01 us
    all_to_all x0 -> x1, blocking collectives: none -> 11.9 us  [on_device(): rows = lax.all_to_all(rows, AXIS, split_axis=0, concat_axis=0, tiled=True)]
    all_to_all x1 -> x0, waiting for transfers between devices: 8 us -> none  [on_device(): rows = lax.all_to_all(rows, AXIS, split_axis=0, concat_axis=0, tiled=True)]
    all_to_all x1 -> x0, starting transfers between devices: 3.84 us -> none  [on_device(): rows = lax.all_to_all(rows, AXIS, split_axis=0, concat_axis=0, tiled=True)]
    pallas_call x1, Pallas kernels: 10.2 us -> 7.62 us  [frame_rows(): pl.pallas_call(kernel, out_shape=jax.ShapeDtypeStruct((count, proj.shape[...]
    pallas_call x1, Pallas kernels: 5.31 us -> 4.41 us  [mix_tracks(): pl.pallas_call(kernel, out_shape=jax.ShapeDtypeStruct(rows.shape, rows.dt...]
    all_to_all x2, local copies, waits for them, and re-layouts: 0.73 us -> 0.07 us  [on_device(): rows = lax.all_to_all(rows, AXIS, split_axis=0, concat_axis=0, tiled=True)]
    pallas_call x1 -> x2, Pallas kernels: 2.15 us -> 2.57 us  [the longest x1 1.86 us: conv_tables(): pl.pallas_call(kernel, out_shape=[jax.ShapeDtypeStruct((side // 2 // grid...]
  transfers between devices with their start and end apart: 8 -> 7, of which waited for: 6 -> 5; matrix products, arithmetic and copies ran while one was open for 1% -> 0% of each run, Pallas kernels for 4% -> 5%
where the time goes in v3:
time: 56.9 us; the launch traced here: 56.8 us
  blocking collectives  21.9 us (38%)
  Pallas kernels  16.7 us (29%)
  starting transfers between devices  9.49 us (17%)
  waiting for transfers between devices  6.62 us (12%)
  local copies, waits for them, and re-layouts  1.01 us (2%)
  other arithmetic  0.88 us (2%)
    all_to_all x1, blocking collectives, on_device(): rows = lax.all_to_all(rows, AXIS, split_axis=0, concat_axis=0, tiled=True)  11.9 us
    all_to_all x1, blocking collectives, on_device(): mixed = lax.all_to_all(mixed, AXIS, split_axis=0, concat_axis=0, tiled=True)  10 us
    ppermute x7, starting transfers between devices, exchange(): lax.ppermute(values, AXIS, [(i, i ^ shift) for i in range(devices)])  9.49 us
    pallas_call x1, Pallas kernels, frame_rows(): pl.pallas_call(kernel, out_shape=jax.ShapeDtypeStruct((count, proj.shape[...  7.62 us
    ppermute x7, waiting for transfers between devices, exchange(): lax.ppermute(values, AXIS, [(i, i ^ shift) for i in range(devices)])  6.62 us
    pallas_call x1, Pallas kernels, mix_tracks(): pl.pallas_call(kernel, out_shape=jax.ShapeDtypeStruct(rows.shape, rows.dt...  4.41 us
    pallas_call x1, Pallas kernels, pick_queries(): pl.pallas_call(kernel, out_shape=jax.ShapeDtypeStruct((count, channels),...  2.14 us
    pallas_call x1, Pallas kernels, conv_tables(): pl.pallas_call(kernel, out_shape=[jax.ShapeDtypeStruct((side // 2 // grid...  1.86 us
  transfers between devices with their start and end apart: 7, of which 5 were waited for; matrix products, arithmetic and copies ran while one was open for 0% of the time, Pallas kernels for 5%

profile of v3, /device:TPU:0, one launch (start us, length us, event | category | flops | bytes accessed | tf_op | source)
XLA Modules:
  0.0 56.8 jit_solution(2805602181754343075)
XLA Ops:
  0.0 0.0 copy-start.1
  0.0 0.0 copy-start.6
  0.0 0.0 copy-start.3
  0.0 0.0 copy-start.7
  0.0 0.8 %fusion.refs_0_ = s32[1,128]{1,0:T(1,128)S(1)} fusion(s32[128]{0:T(128)} %param.14, s32[128]{0:T(128)} %param.13, s32[]{:T(128)S(6)} %axis_index.12), kind=kLoop, calls=%fused_computation.3 | loop fusion | flops 256 | bytes 1540 | tf_op jit(solution)/shard_map/reshape | solution.py:89
  0.8 2.1 %pick_queries.1 = bf16[128,256]{1,0:T(8,128)(2,1)S(1)} custom-call(s32[1,128]{1,0:T(1,128)S(1)} %fusion.refs_0_, bf16[1,4096,256]{2,1,0:T(8,128)(2,1)} %refs_1_.3), custom_call_target="tpu_custom_call" | custom-call | tf_op jit(solution)/shard_map/pick_queries/pallas_call | solution.py:78
  3.0 0.5 collective-permute-start
  3.5 0.9 %collective-permute-done = bf16[128,256]{1,0:T(8,128)(2,1)S(1)} collective-permute-done((bf16[128,256]{1,0:T(8,128)(2,1)S(1)}, bf16[128,256]{1,0:T(8,128)(2,1)S(1)}, u32[]{:S(2)}, u32[]{:S(2)}) %collective-permute-start) | collective-permute-done | bytes 65568 | tf_op jit(solution)/shard_map/ppermute | solution.py:36
  4.4 3.9 %collective-permute-start.3 = (bf16[128,256]{1,0:T(8,128)(2,1)S(1)}, bf16[128,256]{1,0:T(8,128)(2,1)S(1)}, u32[]{:S(2)}, u32[]{:S(2)}) collective-permute-start(bf16[128,256]{1,0:T(8,128)(2,1)S(1)} %add.21), channel_id=1, source_target_pairs={{0,6},{1,7},{2,4},{3,5},{4,2},{5,3},{6,0},{7,1},{8,14},{9,15},{10,... | collective-permute-start | bytes 196616 | tf_op jit(solution)/shard_map/ppermute | solution.py:36
  8.3 0.5 collective-permute-start.2
  8.8 0.1 collective-permute-start.1
  8.9 0.0 copy-done.1
  8.9 0.0 copy-done.6
  8.9 0.0 copy-done.3
  8.9 1.9 %conv_tables.1 = (bf16[2048,256]{1,0:T(8,128)(2,1)S(1)}, f32[512,128]{1,0:T(8,128)S(1)}, bf16[128,256]{1,0:T(8,128)(2,1)S(1)}) custom-call(f32[16,9]{1,0:T(8,128)S(1)} %copy-done.3, f32[1,16]{1,0:T(1,128)S(1)} %bitcast.16, bf16[64,32]{1,0:T(8,128)(2,1)S(1)} %bitcast.13), custom_call_target="tpu_custom_call" | custom-call | tf_op jit(solution)/shard_map/conv_tables/pallas_call | solution.py:144
  10.8 0.0 collective-permute-done.3
  10.8 1.7 %collective-permute-done.2 = bf16[128,256]{1,0:T(8,128)(2,1)S(1)} collective-permute-done((bf16[128,256]{1,0:T(8,128)(2,1)S(1)}, bf16[128,256]{1,0:T(8,128)(2,1)S(1)}, u32[]{:S(2)}, u32[]{:S(2)}) %collective-permute-start.2) | collective-permute-done | bytes 65568 | tf_op jit(solution)/shard_map/ppermute | solution.py:36
  12.6 0.5 collective-permute-done.1
  13.1 3.7 %collective-permute-start.6 = (bf16[128,256]{1,0:T(8,128)(2,1)S(1)}, bf16[128,256]{1,0:T(8,128)(2,1)S(1)}, u32[]{:S(2)}, u32[]{:S(2)}) collective-permute-start(bf16[128,256]{1,0:T(8,128)(2,1)S(1)} %add_add_fusion.1), channel_id=1, source_target_pairs={{0,24},{1,25},{2,26},{3,27},{4,28},{5,29},{6,30},{7,31},{8,16},{9,... | collective-permute-start | bytes 196616 | tf_op jit(solution)/shard_map/ppermute | solution.py:36
  16.8 0.0 collective-permute-start.5
  16.8 0.8 %collective-permute-start.4 = (bf16[128,256]{1,0:T(8,128)(2,1)S(1)}, bf16[128,256]{1,0:T(8,128)(2,1)S(1)}, u32[]{:S(2)}, u32[]{:S(2)}) collective-permute-start(bf16[128,256]{1,0:T(8,128)(2,1)S(1)} %add_add_fusion.1), channel_id=1, source_target_pairs={{0,8},{1,9},{2,10},{3,11},{4,12},{5,13},{6,14},{7,15},{8,0},{9,1},... | collective-permute-start | bytes 196616 | tf_op jit(solution)/shard_map/ppermute | solution.py:36
  17.5 0.0 copy-done.7
  17.5 0.2 copy.13
  17.7 0.0 copy-start
  17.7 0.7 %order_proj.1.refs_5_ = bf16[2048,512]{1,0:T(8,128)(2,1)S(1)} custom-call(bf16[2048,512]{1,0:T(8,128)(2,1)S(1)} %bitcast.12), custom_call_target="tpu_custom_call" | custom-call | tf_op jit(solution)/shard_map/order_proj/pallas_call | solution.py:184
  18.5 0.8 %collective-permute-done.6 = bf16[128,256]{1,0:T(8,128)(2,1)S(1)} collective-permute-done((bf16[128,256]{1,0:T(8,128)(2,1)S(1)}, bf16[128,256]{1,0:T(8,128)(2,1)S(1)}, u32[]{:S(2)}, u32[]{:S(2)}) %collective-permute-start.6) | collective-permute-done | bytes 65568 | tf_op jit(solution)/shard_map/ppermute | solution.py:36
  19.2 2.7 %collective-permute-done.5 = bf16[128,256]{1,0:T(8,128)(2,1)S(1)} collective-permute-done((bf16[128,256]{1,0:T(8,128)(2,1)S(1)}, bf16[128,256]{1,0:T(8,128)(2,1)S(1)}, u32[]{:S(2)}, u32[]{:S(2)}) %collective-permute-start.5) | collective-permute-done | bytes 65568 | tf_op jit(solution)/shard_map/ppermute | solution.py:36
  21.9 0.0 collective-permute-done.4
  21.9 0.0 copy-done
  22.0 0.0 copy-start.2
  22.0 0.0 copy-start.4
  22.0 0.0 copy-start.5
  22.0 7.6 %frame_rows.1 = bf16[128,512]{1,0:T(8,128)(2,1)S(1)} custom-call(bf16[128,256]{1,0:T(8,128)(2,1)S(1)} %add_add_fusion.refs_0_, bf16[1,4096,256]{2,1,0:T(8,128)(2,1)S(1)} %copy-done, bf16[2048,256]{1,0:T(8,128)(2,1)S(1)} %get-tuple-element.25.refs_2_, f32[512,128]{1,0:T(8,128)S(1)} %get-tuple-element.26.refs_3_, ...), custom_call_target="tpu_custom_call" | custom-call | tf_op jit(solution)/shard_map/frame_rows/pallas_call | solution.py:270
  29.7 11.9 %all_to_all.20 = bf16[32,4,512]{2,1,0:T(4,128)(2,1)S(1)} all-to-all(bf16[32,4,512]{2,1,0:T(4,128)(2,1)S(1)} %all_to_all.13), channel_id=1, replica_groups=mesh['groups'=1,'frames'=32] {'frames'}, dimensions={0} | all-to-all | bytes 262144 | tf_op jit(solution)/shard_map/all_to_all | solution.py:408
  41.6 0.0 copy-done.2
  41.6 0.0 copy-done.4
  41.6 0.0 copy-done.5
  41.6 4.4 %mixer.1 = bf16[128,512]{1,0:T(8,128)(2,1)S(1)} custom-call(bf16[128,512]{1,0:T(8,128)(2,1)S(1)} %all_to_all.15.refs_0_, s32[1,32]{1,0:T(1,128)S(1)} %bitcast.15, f32[2,2,512]{2,1,0:T(2,128)S(1)} %copy-done.4, f32[3,2,512]{2,1,0:T(2,128)S(1)} %bitcast.14, bf16[2,512,2048]{2,1,0:T(8,128)(2,1)} %refs_4_.1, bf16[2,2048,512]{2,1,0:T(8,128)(2,1)} %refs_5_.1), custom_call_target="tpu_custom_call" | custom-call | tf_op jit(solution)/shard_map/mixer/pallas_call | solution.py:356
  46.1 10.0 %all_to_all.21 = bf16[32,4,512]{2,1,0:T(4,128)(2,1)S(1)} all-to-all(bf16[32,4,512]{2,1,0:T(4,128)(2,1)S(1)} %all_to_all.16), channel_id=1, replica_groups=mesh['groups'=1,'frames'=32] {'frames'}, dimensions={0} | all-to-all | bytes 262144 | tf_op jit(solution)/shard_map/all_to_all | solution.py:411
  56.1 0.7 %broadcast_in_dim.8 = bf16[1,128,512]{2,1,0:T(8,128)(2,1)} reshape(bf16[32,4,512]{2,1,0:T(4,128)(2,1)S(1)} %all_to_all.21) | data formatting | bytes 262144 | tf_op jit(solution)/shard_map/broadcast_in_dim | solution.py:412
  (6 shorter events, 0.2 us)
Async XLA Ops:
  0.0 8.9 %copy-start.1 = (bf16[32,16,2,2]{0,3,2,1:T(2,128)(2,1)S(1)}, bf16[32,16,2,2]{0,3,2,1:T(2,128)(2,1)}, u32[]{:S(2)}) copy-start(bf16[32,16,2,2]{0,3,2,1:T(2,128)(2,1)} %param.18) | copy-start | bytes 12292
  0.0 8.9 %copy-start.6 = (f32[16]{0:T(128)S(1)}, f32[16]{0:T(128)}, u32[]{:S(2)}) copy-start(f32[16]{0:T(128)} %param.17) | copy-start | bytes 196
  0.0 8.9 %copy-start.3 = (f32[16,9]{1,0:T(8,128)S(1)}, f32[16,9]{1,0:T(8,128)}, u32[]{:S(2)}) copy-start(f32[16,9]{1,0:T(8,128)} %refs_0_) | copy-start | bytes 1732
  0.0 17.5 %copy-start.7 = (bf16[2048,512]{1,0:T(8,128)(2,1)S(1)}, bf16[2048,512]{1,0:T(8,128)(2,1)}, u32[]{:S(2)}) copy-start(bf16[2048,512]{1,0:T(8,128)(2,1)} %param.19) | copy-start | bytes 6291460
  3.0 1.4 %collective-permute-start = (bf16[128,256]{1,0:T(8,128)(2,1)S(1)}, bf16[128,256]{1,0:T(8,128)(2,1)S(1)}, u32[]{:S(2)}, u32[]{:S(2)}) collective-permute-start(bf16[128,256]{1,0:T(8,128)(2,1)S(1)} %pick_queries.1), channel_id=1, source_target_pairs={{0,1},{1,0},{2,3},{3,2},{4,5},{5,4},{6,7},{7,6},{8,9},{9,8},{10,11... | collective-permute-start | bytes 196616 | tf_op jit(solution)/shard_map/ppermute | solution.py:36
  4.4 6.4 %collective-permute-start.3 = (bf16[128,256]{1,0:T(8,128)(2,1)S(1)}, bf16[128,256]{1,0:T(8,128)(2,1)S(1)}, u32[]{:S(2)}, u32[]{:S(2)}) collective-permute-start(bf16[128,256]{1,0:T(8,128)(2,1)S(1)} %add.21), channel_id=1, source_target_pairs={{0,6},{1,7},{2,4},{3,5},{4,2},{5,3},{6,0},{7,1},{8,14},{9,15},{10,... | collective-permute-start | bytes 196616 | tf_op jit(solution)/shard_map/ppermute | solution.py:36
  8.3 4.3 %collective-permute-start.2 = (bf16[128,256]{1,0:T(8,128)(2,1)S(1)}, bf16[128,256]{1,0:T(8,128)(2,1)S(1)}, u32[]{:S(2)}, u32[]{:S(2)}) collective-permute-start(bf16[128,256]{1,0:T(8,128)(2,1)S(1)} %add.21), channel_id=1, source_target_pairs={{0,4},{1,5},{2,6},{3,7},{4,0},{5,1},{6,2},{7,3},{8,12},{9,13},{10,... | collective-permute-start | bytes 196616 | tf_op jit(solution)/shard_map/ppermute | solution.py:36
  8.8 4.3 %collective-permute-start.1 = (bf16[128,256]{1,0:T(8,128)(2,1)S(1)}, bf16[128,256]{1,0:T(8,128)(2,1)S(1)}, u32[]{:S(2)}, u32[]{:S(2)}) collective-permute-start(bf16[128,256]{1,0:T(8,128)(2,1)S(1)} %add.21), channel_id=1, source_target_pairs={{0,2},{1,3},{2,0},{3,1},{4,6},{5,7},{6,4},{7,5},{8,10},{9,11},{10,... | collective-permute-start | bytes 196616 | tf_op jit(solution)/shard_map/ppermute | solution.py:36
  13.1 6.1 %collective-permute-start.6 = (bf16[128,256]{1,0:T(8,128)(2,1)S(1)}, bf16[128,256]{1,0:T(8,128)(2,1)S(1)}, u32[]{:S(2)}, u32[]{:S(2)}) collective-permute-start(bf16[128,256]{1,0:T(8,128)(2,1)S(1)} %add_add_fusion.1), channel_id=1, source_target_pairs={{0,24},{1,25},{2,26},{3,27},{4,28},{5,29},{6,30},{7,31},{8,16},{9,... | collective-permute-start | bytes 196616 | tf_op jit(solution)/shard_map/ppermute | solution.py:36
  16.8 5.2 %collective-permute-start.5 = (bf16[128,256]{1,0:T(8,128)(2,1)S(1)}, bf16[128,256]{1,0:T(8,128)(2,1)S(1)}, u32[]{:S(2)}, u32[]{:S(2)}) collective-permute-start(bf16[128,256]{1,0:T(8,128)(2,1)S(1)} %add_add_fusion.1), channel_id=1, source_target_pairs={{0,16},{1,17},{2,18},{3,19},{4,20},{5,21},{6,22},{7,23},{8,24},{9,... | collective-permute-start | bytes 196616 | tf_op jit(solution)/shard_map/ppermute | solution.py:36
  16.8 5.2 %collective-permute-start.4 = (bf16[128,256]{1,0:T(8,128)(2,1)S(1)}, bf16[128,256]{1,0:T(8,128)(2,1)S(1)}, u32[]{:S(2)}, u32[]{:S(2)}) collective-permute-start(bf16[128,256]{1,0:T(8,128)(2,1)S(1)} %add_add_fusion.1), channel_id=1, source_target_pairs={{0,8},{1,9},{2,10},{3,11},{4,12},{5,13},{6,14},{7,15},{8,0},{9,1},... | collective-permute-start | bytes 196616 | tf_op jit(solution)/shard_map/ppermute | solution.py:36
  17.7 4.2 %copy-start = (bf16[1,4096,256]{2,1,0:T(8,128)(2,1)S(1)}, bf16[1,4096,256]{2,1,0:T(8,128)(2,1)}, u32[]{:S(2)}) copy-start(bf16[1,4096,256]{2,1,0:T(8,128)(2,1)} %refs_1_.3) | copy-start | bytes 6291460
  22.0 19.6 %copy-start.2 = (f32[2,3,512]{2,0,1:T(2,128)S(1)}, f32[2,3,512]{2,0,1:T(2,128)}, u32[]{:S(2)}) copy-start(f32[2,3,512]{2,0,1:T(2,128)} %param.21) | copy-start | bytes 36868
  22.0 19.6 %copy-start.4 = (f32[2,2,512]{2,1,0:T(2,128)S(1)}, f32[2,2,512]{2,1,0:T(2,128)}, u32[]{:S(2)}) copy-start(f32[2,2,512]{2,1,0:T(2,128)} %refs_2_.1) | copy-start | bytes 24580
  22.0 19.6 %copy-start.5 = (s32[32]{0:T(128)S(1)}, s32[32]{0:T(128)}, u32[]{:S(2)}) copy-start(s32[32]{0:T(128)} %param.15) | copy-start | bytes 388

commit v4 on v3

--- a/solution.py
+++ b/solution.py
@@ -21,12 +21,9 @@
 
 def exchange_stages(devices):
     stages = []
-    bit = 1
+    bit = 2
     while bit < devices:
-        if bit == 1 or 2 * bit >= devices:
-            stages.append((bit,))
-        else:
-            stages.append((bit, 2 * bit, 3 * bit))
+        stages.append((bit,) if 2 * bit >= devices else (bit, 2 * bit, 3 * bit))
         bit *= len(stages[-1]) + 1
     return stages
 
@@ -40,51 +37,30 @@
     return values
 
 
-def pick_kernel(pieces, wanted_ref, feat_hbm, out_ref, feat, sems):
-    points, channels = feat.shape
+def pick_kernel(wanted_ref, feat_ref, mine_ref, other_ref):
+    points = feat_ref.shape[1]
     count = wanted_ref.shape[1]
-    piece = points // pieces
-    copies = [
-        pltpu.make_async_copy(
-            feat_hbm.at[0, pl.ds(n * piece, piece)], feat.at[pl.ds(n * piece, piece)], sems.at[n]
-        )
-        for n in range(pieces)
-    ]
-    for copy in copies:
-        copy.start()
     wanted = jnp.broadcast_to(wanted_ref[...], (count, count)).T
-    total = jnp.zeros((count, channels), jnp.float32)
-    for n in range(pieces):
-        parts = []
-        for at in range(n * piece, (n + 1) * piece, count):
-            parts.append((wanted == iota((count, count), 1) + at).astype(jnp.bfloat16))
-        hot = jnp.concatenate(parts, axis=1)
-        copies[n].wait()
-        total = total + jnp.dot(
-            hot, feat[n * piece : (n + 1) * piece], preferred_element_type=jnp.float32
-        )
-    out_ref[...] = total.astype(out_ref.dtype)
+    spots = iota((count, count), 1)
+    hot = jnp.concatenate(
+        [(wanted == spots + at).astype(jnp.bfloat16) for at in range(0, points, count)], axis=1
+    )
+    total = jnp.dot(hot, feat_ref[0], preferred_element_type=jnp.float32).astype(mine_ref.dtype)
+    low, high = total[: count // 2], total[count // 2 :]
+    even = lax.axis_index(AXIS) % 2 == 0
+    mine_ref[...] = jnp.where(even, low, high)
+    other_ref[...] = jnp.where(even, high, low)
 
 
 def pick_queries(features, query_frame, query_pos):
-    points, channels = features.shape[1:]
     count = query_frame.shape[0]
     wanted = jnp.where(query_frame == lax.axis_index(AXIS), query_pos, -1)
-    pieces = 4
-
-    def kernel(*refs):
-        pick_kernel(pieces, *refs)
-
     return pl.pallas_call(
-        kernel,
-        out_shape=jax.ShapeDtypeStruct((count, channels), features.dtype),
-        in_specs=[VMEM, HBM],
-        out_specs=VMEM,
-        scratch_shapes=[
-            pltpu.VMEM((points, channels), features.dtype),
-            pltpu.SemaphoreType.DMA((pieces,)),
-        ],
-        compiler_params=pltpu.CompilerParams(vmem_limit_bytes=53 * MIB),
+        pick_kernel,
+        out_shape=[jax.ShapeDtypeStruct((count // 2, features.shape[2]), features.dtype)] * 2,
+        in_specs=[VMEM, VMEM],
+        out_specs=[VMEM, VMEM],
+        compiler_params=pltpu.CompilerParams(vmem_limit_bytes=16 * MIB),
         name="pick_queries",
     )(wanted.reshape(1, -1), features)
 
@@ -192,19 +168,21 @@
 
 
 def rows_kernel(
-    side, grid, query_ref, feat_ref, first_ref, bias_ref, second_ref, proj_ref, out_ref,
+    side, grid, mine_ref, other_ref, feat_ref, first_ref, bias_ref, second_ref, proj_ref, out_ref,
     corr, hold,
 ):
     half = side // 2
     width = half // grid
-    count, channels = query_ref.shape
+    mine, other = mine_ref[...], other_ref[...]
+    even = lax.axis_index(AXIS) % 2 == 0
+    query = jnp.concatenate([jnp.where(even, mine, other), jnp.where(even, other, mine)], axis=0)
+    count, channels = query.shape
     points = feat_ref.shape[1]
     scale = 1.0 / math.sqrt(channels)
     step = 2 * side
     edge = jnp.zeros((side, count), corr.dtype)
     corr[pl.ds(0, side)] = edge
     corr[pl.ds(side + points, side)] = edge
-    query = query_ref[...]
     piece = min(512, points)
     for at in range(0, points, piece):
         part = lax.dot_general(
@@ -261,8 +239,8 @@
     out_ref[...] = total.astype(out_ref.dtype)
 
 
-def frame_rows(queries, features, tables, proj, side, grid):
-    count = queries.shape[0]
+def frame_rows(mine, other, features, tables, proj, side, grid):
+    count = 2 * mine.shape[0]
 
     def kernel(*refs):
         rows_kernel(side, grid, *refs)
@@ -270,7 +248,7 @@
     return pl.pallas_call(
         kernel,
         out_shape=jax.ShapeDtypeStruct((count, proj.shape[1]), jnp.bfloat16),
-        in_specs=[VMEM] * 6,
+        in_specs=[VMEM] * 7,
         out_specs=VMEM,
         scratch_shapes=[
             pltpu.VMEM((features.shape[1] + 2 * side, count), jnp.bfloat16),
@@ -278,7 +256,7 @@
         ],
         compiler_params=pltpu.CompilerParams(vmem_limit_bytes=32 * MIB),
         name="frame_rows",
-    )(queries, features, *tables, proj)
+    )(mine, other, features, *tables, proj)
 
 
 def layer_norm(values):
@@ -387,24 +365,32 @@
     side = math.isqrt(features.shape[1])
     grid = math.isqrt(proj_weight.shape[0] // conv2_weight.shape[0])
 
-    queries = pick_queries(features, query_frame, query_pos)
+    mine, other = pick_queries(features, query_frame, query_pos)
     ch1, ch2 = conv1_weight.shape[0], conv2_weight.shape[0]
     convs = (conv1_weight, conv1_bias, conv2_weight)
     if devices & (devices - 1):
-        queries = lax.psum(queries, AXIS)
+        even = lax.axis_index(AXIS) % 2 == 0
+        half = mine.shape[0]
+        both = jnp.concatenate([jnp.where(even, mine, other), jnp.where(even, other, mine)], axis=0)
+        both = lax.psum(both, AXIS)
+        mine = jnp.where(even, both[:half], both[half:])
+        other = jnp.where(even, both[half:], both[:half])
         tables = conv_tables(*convs, side, grid)
         proj = order_proj(proj_weight, ch1, ch2, grid)
     else:
+        swap = [(i, i ^ 1) for i in range(devices)]
+        mine = mine + lax.ppermute(other, AXIS, swap)
+        mine, convs = lax.optimization_barrier((mine, convs))
+        tables = conv_tables(*convs, side, grid)
         stages = exchange_stages(devices)
-        queries = exchange(queries, stages[0], devices)
-        queries, convs = lax.optimization_barrier((queries, convs))
-        tables = conv_tables(*convs, side, grid)
-        queries = exchange(queries, stages[1], devices)
-        queries, tables, proj_weight = lax.optimization_barrier((queries, tables, proj_weight))
+        mine = exchange(mine, stages[0], devices)
+        mine, tables, proj_weight = lax.optimization_barrier((mine, tables, proj_weight))
         proj = order_proj(proj_weight, ch1, ch2, grid)
-        for shifts in stages[2:]:
-            queries = exchange(queries, shifts, devices)
-    rows = frame_rows(queries, features, tables, proj, side, grid)
+        for shifts in stages[1:]:
+            mine = exchange(mine, shifts, devices)
+        mine, proj = lax.optimization_barrier((mine, proj))
+        other = lax.ppermute(mine, AXIS, swap)
+    rows = frame_rows(mine, other, features, tables, proj, side, grid)
     rows = lax.all_to_all(rows, AXIS, split_axis=0, concat_axis=0, tiled=True)
     place = frame_order.reshape(1, -1)
     mixed = mix_tracks(rows, place, norm_gains, time_kernels.transpose(1, 0, 2), mix_up, mix_down, tracks)

time: 56.9 us -> 56.7 us (level)
  Pallas kernels: 16.7 us -> 15.1 us
  local copies, waits for them, and re-layouts: 1.01 us -> 2.6 us
    ppermute x0 -> x2, waiting for transfers between devices: none -> 2.05 us  [the longest x1 1.19 us: on_device(): other = lax.ppermute(mine, AXIS, swap)]
    pallas_call x1, Pallas kernels: 2.14 us -> 0.48 us  [pick_queries(): pl.pallas_call(pick_kernel, out_shape=[jax.ShapeDtypeStruct((count // 2,...]
    ppermute x7 -> x6, waiting for transfers between devices: 6.62 us -> 5.02 us  [exchange(): lax.ppermute(values, AXIS, [(i, i ^ shift) for i in range(devices)])]
    unnamed x16 -> x18, local copies, waits for them, and re-layouts: 0.04 us -> 1.63 us
    ppermute x0 -> x2, starting transfers between devices: none -> 0.59 us  [the longest x1 0.52 us: on_device(): mine = mine + lax.ppermute(other, AXIS, swap)]
    ppermute x7 -> x6, starting transfers between devices: 9.49 us -> 8.95 us  [exchange(): lax.ppermute(values, AXIS, [(i, i ^ shift) for i in range(devices)])]
  transfers between devices with their start and end apart: 7 -> 8, of which waited for: 5 -> 6; matrix products, arithmetic and copies ran while one was open for 0% -> 0% of each run, Pallas kernels for 5% -> 5%
where the time goes in v4:
time: 56.7 us; the launch traced here: 56.5 us
  blocking collectives  21.4 us (38%)
  Pallas kernels  15.1 us (27%)
  starting transfers between devices  9.54 us (17%)
  waiting for transfers between devices  7.07 us (12%)
  local copies, waits for them, and re-layouts  2.6 us (5%)
  other arithmetic  0.72 us (1%)
    all_to_all x1, blocking collectives, on_device(): rows = lax.all_to_all(rows, AXIS, split_axis=0, concat_axis=0, tiled=True)  11.4 us
    all_to_all x1, blocking collectives, on_device(): mixed = lax.all_to_all(mixed, AXIS, split_axis=0, concat_axis=0, tiled=True)  10 us
    ppermute x6, starting transfers between devices, exchange(): lax.ppermute(values, AXIS, [(i, i ^ shift) for i in range(devices)])  8.95 us
    pallas_call x1, Pallas kernels, frame_rows(): pl.pallas_call(kernel, out_shape=jax.ShapeDtypeStruct((count, proj.shape[...  7.64 us
    ppermute x6, waiting for transfers between devices, exchange(): lax.ppermute(values, AXIS, [(i, i ^ shift) for i in range(devices)])  5.02 us
    pallas_call x1, Pallas kernels, mix_tracks(): pl.pallas_call(kernel, out_shape=jax.ShapeDtypeStruct(rows.shape, rows.dt...  4.41 us
    pallas_call x1, Pallas kernels, conv_tables(): pl.pallas_call(kernel, out_shape=[jax.ShapeDtypeStruct((side // 2 // grid...  1.86 us
    unnamed x18, local copies, waits for them, and re-layouts  1.63 us
  transfers between devices with their start and end apart: 8, of which 6 were waited for; matrix products, arithmetic and copies ran while one was open for 0% of the time, Pallas kernels for 5%

profile of v4, /device:TPU:0, one launch (start us, length us, event | category | flops | bytes accessed | tf_op | source)
XLA Modules:
  0.0 56.5 jit_solution(6163831805283624364)
XLA Ops:
  0.0 0.0 copy-start.7
  0.0 0.7 %fusion.wanted_ref = s32[1,128]{1,0:T(1,128)S(1)} fusion(s32[128]{0:T(128)} %param.14, s32[128]{0:T(128)} %param.13, s32[]{:T(128)S(6)} %axis_index.12), kind=kLoop, calls=%fused_computation.3 | loop fusion | flops 256 | bytes 1540 | tf_op jit(solution)/shard_map/reshape | solution.py:65
  0.7 0.0 copy-start
  0.7 1.6 %copy-done = bf16[1,4096,256]{2,1,0:T(8,128)(2,1)S(1)} copy-done((bf16[1,4096,256]{2,1,0:T(8,128)(2,1)S(1)}, bf16[1,4096,256]{2,1,0:T(8,128)(2,1)}, u32[]{:S(2)}) %copy-start) | copy-done | bytes 2097176
  2.3 0.0 copy-start.2
  2.3 0.0 copy-start.4
  2.3 0.0 copy-start.8
  2.3 0.5 pick_queries.1
  2.8 0.5 collective-permute-start
  3.3 0.9 %collective-permute-done = bf16[64,256]{1,0:T(8,128)(2,1)S(1)} collective-permute-done((bf16[64,256]{1,0:T(8,128)(2,1)S(1)}, bf16[64,256]{1,0:T(8,128)(2,1)S(1)}, u32[]{:S(2)}, u32[]{:S(2)}) %collective-permute-start) | collective-permute-done | bytes 32800 | tf_op jit(solution)/shard_map/ppermute | solution.py:382
  4.2 3.9 %collective-permute-start.3 = (bf16[64,256]{1,0:T(8,128)(2,1)S(1)}, bf16[64,256]{1,0:T(8,128)(2,1)S(1)}, u32[]{:S(2)}, u32[]{:S(2)}) collective-permute-start(bf16[64,256]{1,0:T(8,128)(2,1)S(1)} %add.21), channel_id=1, source_target_pairs={{0,6},{1,7},{2,4},{3,5},{4,2},{5,3},{6,0},{7,1},{8,14},{9,15},{10,... | collective-permute-start | bytes 98312 | tf_op jit(solution)/shard_map/ppermute | solution.py:33
  8.0 0.5 collective-permute-start.2
  8.5 0.1 collective-permute-start.1
  8.7 0.0 copy-done.7
  8.7 0.0 copy-done.2
  8.7 0.0 copy-done.4
  8.7 1.9 %conv_tables.1 = (bf16[2048,256]{1,0:T(8,128)(2,1)S(1)}, f32[512,128]{1,0:T(8,128)S(1)}, bf16[128,256]{1,0:T(8,128)(2,1)S(1)}) custom-call(f32[16,9]{1,0:T(8,128)S(1)} %copy-done.4, f32[1,16]{1,0:T(1,128)S(1)} %bitcast.16, bf16[64,32]{1,0:T(8,128)(2,1)S(1)} %bitcast.13), custom_call_target="tpu_custom_call" | custom-call | tf_op jit(solution)/shard_map/conv_tables/pallas_call | solution.py:120
  10.5 0.0 collective-permute-done.3
  10.6 1.4 %collective-permute-done.2 = bf16[64,256]{1,0:T(8,128)(2,1)S(1)} collective-permute-done((bf16[64,256]{1,0:T(8,128)(2,1)S(1)}, bf16[64,256]{1,0:T(8,128)(2,1)S(1)}, u32[]{:S(2)}, u32[]{:S(2)}) %collective-permute-start.2) | collective-permute-done | bytes 32800 | tf_op jit(solution)/shard_map/ppermute | solution.py:33
  11.9 0.5 collective-permute-done.1
  12.5 3.7 %collective-permute-start.6 = (bf16[64,256]{1,0:T(8,128)(2,1)S(1)}, bf16[64,256]{1,0:T(8,128)(2,1)S(1)}, u32[]{:S(2)}, u32[]{:S(2)}) collective-permute-start(bf16[64,256]{1,0:T(8,128)(2,1)S(1)} %add_add_fusion.1), channel_id=1, source_target_pairs={{0,24},{1,25},{2,26},{3,27},{4,28},{5,29},{6,30},{7,31},{8,16},{9,... | collective-permute-start | bytes 98312 | tf_op jit(solution)/shard_map/ppermute | solution.py:33
  16.1 0.0 collective-permute-start.5
  16.1 0.8 %collective-permute-start.4 = (bf16[64,256]{1,0:T(8,128)(2,1)S(1)}, bf16[64,256]{1,0:T(8,128)(2,1)S(1)}, u32[]{:S(2)}, u32[]{:S(2)}) collective-permute-start(bf16[64,256]{1,0:T(8,128)(2,1)S(1)} %add_add_fusion.1), channel_id=1, source_target_pairs={{0,8},{1,9},{2,10},{3,11},{4,12},{5,13},{6,14},{7,15},{8,0},{9,1},... | collective-permute-start | bytes 98312 | tf_op jit(solution)/shard_map/ppermute | solution.py:33
  16.9 0.0 copy-done.8
  16.9 0.2 copy.13
  17.1 0.0 copy-start.1
  17.1 0.7 %order_proj.1.refs_6_ = bf16[2048,512]{1,0:T(8,128)(2,1)S(1)} custom-call(bf16[2048,512]{1,0:T(8,128)(2,1)S(1)} %bitcast.12), custom_call_target="tpu_custom_call" | custom-call | tf_op jit(solution)/shard_map/order_proj/pallas_call | solution.py:160
  17.8 0.5 collective-permute-done.6
  18.3 2.6 %collective-permute-done.5 = bf16[64,256]{1,0:T(8,128)(2,1)S(1)} collective-permute-done((bf16[64,256]{1,0:T(8,128)(2,1)S(1)}, bf16[64,256]{1,0:T(8,128)(2,1)S(1)}, u32[]{:S(2)}, u32[]{:S(2)}) %collective-permute-start.5) | collective-permute-done | bytes 32800 | tf_op jit(solution)/shard_map/ppermute | solution.py:33
  20.9 0.0 collective-permute-done.4
  21.0 0.0 copy-start.3
  21.0 0.0 copy-start.5
  21.0 0.0 copy-start.6
  21.0 0.1 collective-permute-start.7
  21.1 1.2 %collective-permute-done.7.refs_1_ = bf16[64,256]{1,0:T(8,128)(2,1)S(1)} collective-permute-done((bf16[64,256]{1,0:T(8,128)(2,1)S(1)}, bf16[64,256]{1,0:T(8,128)(2,1)S(1)}, u32[]{:S(2)}, u32[]{:S(2)}) %collective-permute-start.7) | collective-permute-done | bytes 32800 | tf_op jit(solution)/shard_map/ppermute | solution.py:392
  22.3 0.0 copy-done.1
  22.3 7.6 %frame_rows.1 = bf16[128,512]{1,0:T(8,128)(2,1)S(1)} custom-call(bf16[64,256]{1,0:T(8,128)(2,1)S(1)} %add_add_fusion.refs_0_, bf16[64,256]{1,0:T(8,128)(2,1)S(1)} %collective-permute-done.7.refs_1_, bf16[1,4096,256]{2,1,0:T(8,128)(2,1)S(1)} %copy-done.1, bf16[2048,256]{1,0:T(8,128)(2,1)S(1)} %get-tuple-element.33.refs_3_, ...), custom_call_target="tpu_custom_call" | custom-call | tf_op jit(solution)/shard_map/frame_rows/pallas_call | solution.py:248
  30.0 11.4 %all_to_all.20 = bf16[32,4,512]{2,1,0:T(4,128)(2,1)S(1)} all-to-all(bf16[32,4,512]{2,1,0:T(4,128)(2,1)S(1)} %all_to_all.13), channel_id=1, replica_groups=mesh['groups'=1,'frames'=32] {'frames'}, dimensions={0} | all-to-all | bytes 262144 | tf_op jit(solution)/shard_map/all_to_all | solution.py:394
  41.4 0.0 copy-done.3
  41.4 0.0 copy-done.5
  41.4 0.0 copy-done.6
  41.4 4.4 %mixer.1 = bf16[128,512]{1,0:T(8,128)(2,1)S(1)} custom-call(bf16[128,512]{1,0:T(8,128)(2,1)S(1)} %all_to_all.15.refs_0_, s32[1,32]{1,0:T(1,128)S(1)} %bitcast.15, f32[2,2,512]{2,1,0:T(2,128)S(1)} %copy-done.5, f32[3,2,512]{2,1,0:T(2,128)S(1)} %bitcast.14, bf16[2,512,2048]{2,1,0:T(8,128)(2,1)} %refs_4_.1, bf16[2,2048,512]{2,1,0:T(8,128)(2,1)} %refs_5_.1), custom_call_target="tpu_custom_call" | custom-call | tf_op jit(solution)/shard_map/mixer/pallas_call | solution.py:334
  45.9 10.0 %all_to_all.21 = bf16[32,4,512]{2,1,0:T(4,128)(2,1)S(1)} all-to-all(bf16[32,4,512]{2,1,0:T(4,128)(2,1)S(1)} %all_to_all.16), channel_id=1, replica_groups=mesh['groups'=1,'frames'=32] {'frames'}, dimensions={0} | all-to-all | bytes 262144 | tf_op jit(solution)/shard_map/all_to_all | solution.py:397
  55.9 0.7 %broadcast_in_dim.8 = bf16[1,128,512]{2,1,0:T(8,128)(2,1)} reshape(bf16[32,4,512]{2,1,0:T(4,128)(2,1)S(1)} %all_to_all.21) | data formatting | bytes 262144 | tf_op jit(solution)/shard_map/broadcast_in_dim | solution.py:398
  (6 shorter events, 0.1 us)
Async XLA Ops:
  0.0 8.7 %copy-start.7 = (f32[16]{0:T(128)S(1)}, f32[16]{0:T(128)}, u32[]{:S(2)}) copy-start(f32[16]{0:T(128)} %param.17) | copy-start | bytes 196
  0.7 1.6 %copy-start = (bf16[1,4096,256]{2,1,0:T(8,128)(2,1)S(1)}, bf16[1,4096,256]{2,1,0:T(8,128)(2,1)}, u32[]{:S(2)}) copy-start(bf16[1,4096,256]{2,1,0:T(8,128)(2,1)} %refs_2_.2) | copy-start | bytes 6291460
  2.3 6.4 %copy-start.2 = (bf16[32,16,2,2]{0,3,2,1:T(2,128)(2,1)S(1)}, bf16[32,16,2,2]{0,3,2,1:T(2,128)(2,1)}, u32[]{:S(2)}) copy-start(bf16[32,16,2,2]{0,3,2,1:T(2,128)(2,1)} %param.18) | copy-start | bytes 12292
  2.3 6.4 %copy-start.4 = (f32[16,9]{1,0:T(8,128)S(1)}, f32[16,9]{1,0:T(8,128)}, u32[]{:S(2)}) copy-start(f32[16,9]{1,0:T(8,128)} %refs_0_) | copy-start | bytes 1732
  2.3 14.6 %copy-start.8 = (bf16[2048,512]{1,0:T(8,128)(2,1)S(1)}, bf16[2048,512]{1,0:T(8,128)(2,1)}, u32[]{:S(2)}) copy-start(bf16[2048,512]{1,0:T(8,128)(2,1)} %param.19) | copy-start | bytes 6291460
  2.8 1.4 %collective-permute-start = (bf16[64,256]{1,0:T(8,128)(2,1)S(1)}, bf16[64,256]{1,0:T(8,128)(2,1)S(1)}, u32[]{:S(2)}, u32[]{:S(2)}) collective-permute-start(bf16[64,256]{1,0:T(8,128)(2,1)S(1)} %get-tuple-element.22), channel_id=1, source_target_pairs={{0,1},{1,0},{2,3},{3,2},{4,5},{5,4},{6,7},{7,6},{8,9},{9,8},{10,11... | collective-permute-start | bytes 98312 | tf_op jit(solution)/shard_map/ppermute | solution.py:382
  4.2 6.4 %collective-permute-start.3 = (bf16[64,256]{1,0:T(8,128)(2,1)S(1)}, bf16[64,256]{1,0:T(8,128)(2,1)S(1)}, u32[]{:S(2)}, u32[]{:S(2)}) collective-permute-start(bf16[64,256]{1,0:T(8,128)(2,1)S(1)} %add.21), channel_id=1, source_target_pairs={{0,6},{1,7},{2,4},{3,5},{4,2},{5,3},{6,0},{7,1},{8,14},{9,15},{10,... | collective-permute-start | bytes 98312 | tf_op jit(solution)/shard_map/ppermute | solution.py:33
  8.0 3.9 %collective-permute-start.2 = (bf16[64,256]{1,0:T(8,128)(2,1)S(1)}, bf16[64,256]{1,0:T(8,128)(2,1)S(1)}, u32[]{:S(2)}, u32[]{:S(2)}) collective-permute-start(bf16[64,256]{1,0:T(8,128)(2,1)S(1)} %add.21), channel_id=1, source_target_pairs={{0,4},{1,5},{2,6},{3,7},{4,0},{5,1},{6,2},{7,3},{8,12},{9,13},{10,... | collective-permute-start | bytes 98312 | tf_op jit(solution)/shard_map/ppermute | solution.py:33
  8.5 3.9 %collective-permute-start.1 = (bf16[64,256]{1,0:T(8,128)(2,1)S(1)}, bf16[64,256]{1,0:T(8,128)(2,1)S(1)}, u32[]{:S(2)}, u32[]{:S(2)}) collective-permute-start(bf16[64,256]{1,0:T(8,128)(2,1)S(1)} %add.21), channel_id=1, source_target_pairs={{0,2},{1,3},{2,0},{3,1},{4,6},{5,7},{6,4},{7,5},{8,10},{9,11},{10,... | collective-permute-start | bytes 98312 | tf_op jit(solution)/shard_map/ppermute | solution.py:33
  12.5 5.9 %collective-permute-start.6 = (bf16[64,256]{1,0:T(8,128)(2,1)S(1)}, bf16[64,256]{1,0:T(8,128)(2,1)S(1)}, u32[]{:S(2)}, u32[]{:S(2)}) collective-permute-start(bf16[64,256]{1,0:T(8,128)(2,1)S(1)} %add_add_fusion.1), channel_id=1, source_target_pairs={{0,24},{1,25},{2,26},{3,27},{4,28},{5,29},{6,30},{7,31},{8,16},{9,... | collective-permute-start | bytes 98312 | tf_op jit(solution)/shard_map/ppermute | solution.py:33
  16.1 4.8 %collective-permute-start.5 = (bf16[64,256]{1,0:T(8,128)(2,1)S(1)}, bf16[64,256]{1,0:T(8,128)(2,1)S(1)}, u32[]{:S(2)}, u32[]{:S(2)}) collective-permute-start(bf16[64,256]{1,0:T(8,128)(2,1)S(1)} %add_add_fusion.1), channel_id=1, source_target_pairs={{0,16},{1,17},{2,18},{3,19},{4,20},{5,21},{6,22},{7,23},{8,24},{9,... | collective-permute-start | bytes 98312 | tf_op jit(solution)/shard_map/ppermute | solution.py:33
  16.1 4.8 %collective-permute-start.4 = (bf16[64,256]{1,0:T(8,128)(2,1)S(1)}, bf16[64,256]{1,0:T(8,128)(2,1)S(1)}, u32[]{:S(2)}, u32[]{:S(2)}) collective-permute-start(bf16[64,256]{1,0:T(8,128)(2,1)S(1)} %add_add_fusion.1), channel_id=1, source_target_pairs={{0,8},{1,9},{2,10},{3,11},{4,12},{5,13},{6,14},{7,15},{8,0},{9,1},... | collective-permute-start | bytes 98312 | tf_op jit(solution)/shard_map/ppermute | solution.py:33
  17.1 5.2 %copy-start.1 = (bf16[1,4096,256]{2,1,0:T(8,128)(2,1)S(1)}, bf16[1,4096,256]{2,1,0:T(8,128)(2,1)}, u32[]{:S(2)}) copy-start(bf16[1,4096,256]{2,1,0:T(8,128)(2,1)} %refs_2_.2) | copy-start | bytes 6291460
  21.0 20.4 %copy-start.3 = (f32[2,3,512]{2,0,1:T(2,128)S(1)}, f32[2,3,512]{2,0,1:T(2,128)}, u32[]{:S(2)}) copy-start(f32[2,3,512]{2,0,1:T(2,128)} %param.21) | copy-start | bytes 36868
  21.0 20.4 %copy-start.5 = (f32[2,2,512]{2,1,0:T(2,128)S(1)}, f32[2,2,512]{2,1,0:T(2,128)}, u32[]{:S(2)}) copy-start(f32[2,2,512]{2,1,0:T(2,128)} %refs_2_.3) | copy-start | bytes 24580
  21.0 20.4 %copy-start.6 = (s32[32]{0:T(128)S(1)}, s32[32]{0:T(128)}, u32[]{:S(2)}) copy-start(s32[32]{0:T(128)} %param.15) | copy-start | bytes 388
  21.0 1.3 %collective-permute-start.7 = (bf16[64,256]{1,0:T(8,128)(2,1)S(1)}, bf16[64,256]{1,0:T(8,128)(2,1)S(1)}, u32[]{:S(2)}, u32[]{:S(2)}) collective-permute-start(bf16[64,256]{1,0:T(8,128)(2,1)S(1)} %add_add_fusion.refs_0_), channel_id=1, source_target_pairs={{0,1},{1,0},{2,3},{3,2},{4,5},{5,4},{6,7},{7,6},{8,9},{9,8},{10,11... | collective-permute-start | bytes 98312 | tf_op jit(solution)/shard_map/ppermute | solution.py:392

commit v5 on v4

--- a/solution.py
+++ b/solution.py
@@ -23,7 +23,12 @@
     stages = []
     bit = 2
     while bit < devices:
-        stages.append((bit,) if 2 * bit >= devices else (bit, 2 * bit, 3 * bit))
+        if 2 * bit >= devices:
+            stages.append((bit,))
+        elif stages:
+            stages.append((2 * bit, bit, 3 * bit))
+        else:
+            stages.append((bit, 2 * bit, 3 * bit))
         bit *= len(stages[-1]) + 1
     return stages
 

time: 56.7 us -> 56.7 us (level)
  transfers between devices with their start and end apart: 8 -> 8, of which waited for: 6 -> 7; matrix products, arithmetic and copies ran while one was open for 0% -> 0% of each run, Pallas kernels for 5% -> 5%
where the time goes in v5:
time: 56.7 us; the launch traced here: 56.6 us
  blocking collectives  21.4 us (38%)
  Pallas kernels  15.1 us (27%)
  starting transfers between devices  9.54 us (17%)
  waiting for transfers between devices  7.07 us (12%)
  local copies, waits for them, and re-layouts  2.6 us (5%)
  other arithmetic  0.72 us (1%)
    all_to_all x1, blocking collectives, on_device(): rows = lax.all_to_all(rows, AXIS, split_axis=0, concat_axis=0, tiled=True)  11.4 us
    all_to_all x1, blocking collectives, on_device(): mixed = lax.all_to_all(mixed, AXIS, split_axis=0, concat_axis=0, tiled=True)  10 us
    ppermute x6, starting transfers between devices, exchange(): lax.ppermute(values, AXIS, [(i, i ^ shift) for i in range(devices)])  8.95 us
    pallas_call x1, Pallas kernels, frame_rows(): pl.pallas_call(kernel, out_shape=jax.ShapeDtypeStruct((count, proj.shape[...  7.64 us
    ppermute x6, waiting for transfers between devices, exchange(): lax.ppermute(values, AXIS, [(i, i ^ shift) for i in range(devices)])  5.02 us
    pallas_call x1, Pallas kernels, mix_tracks(): pl.pallas_call(kernel, out_shape=jax.ShapeDtypeStruct(rows.shape, rows.dt...  4.4 us
    pallas_call x1, Pallas kernels, conv_tables(): pl.pallas_call(kernel, out_shape=[jax.ShapeDtypeStruct((side // 2 // grid...  1.86 us
    unnamed x18, local copies, waits for them, and re-layouts  1.63 us
  transfers between devices with their start and end apart: 8, of which 7 were waited for; matrix products, arithmetic and copies ran while one was open for 0% of the time, Pallas kernels for 5%

profile of v5, /device:TPU:0, one launch (start us, length us, event | category | flops | bytes accessed | tf_op | source)
XLA Modules:
  0.0 56.6 jit_solution(10123179844508018788)
XLA Ops:
  0.0 0.0 copy-start.7
  0.0 0.7 %fusion.wanted_ref = s32[1,128]{1,0:T(1,128)S(1)} fusion(s32[128]{0:T(128)} %param.14, s32[128]{0:T(128)} %param.13, s32[]{:T(128)S(6)} %axis_index.12), kind=kLoop, calls=%fused_computation.3 | loop fusion | flops 256 | bytes 1540 | tf_op jit(solution)/shard_map/reshape | solution.py:70
  0.7 0.0 copy-start
  0.7 1.6 %copy-done = bf16[1,4096,256]{2,1,0:T(8,128)(2,1)S(1)} copy-done((bf16[1,4096,256]{2,1,0:T(8,128)(2,1)S(1)}, bf16[1,4096,256]{2,1,0:T(8,128)(2,1)}, u32[]{:S(2)}) %copy-start) | copy-done | bytes 2097176
  2.3 0.0 copy-start.2
  2.3 0.0 copy-start.4
  2.3 0.0 copy-start.8
  2.3 0.5 pick_queries.1
  2.8 0.5 collective-permute-start
  3.3 0.9 %collective-permute-done = bf16[64,256]{1,0:T(8,128)(2,1)S(1)} collective-permute-done((bf16[64,256]{1,0:T(8,128)(2,1)S(1)}, bf16[64,256]{1,0:T(8,128)(2,1)S(1)}, u32[]{:S(2)}, u32[]{:S(2)}) %collective-permute-start) | collective-permute-done | bytes 32800 | tf_op jit(solution)/shard_map/ppermute | solution.py:387
  4.2 3.9 %collective-permute-start.3 = (bf16[64,256]{1,0:T(8,128)(2,1)S(1)}, bf16[64,256]{1,0:T(8,128)(2,1)S(1)}, u32[]{:S(2)}, u32[]{:S(2)}) collective-permute-start(bf16[64,256]{1,0:T(8,128)(2,1)S(1)} %add.21), channel_id=1, source_target_pairs={{0,6},{1,7},{2,4},{3,5},{4,2},{5,3},{6,0},{7,1},{8,14},{9,15},{10,... | collective-permute-start | bytes 98312 | tf_op jit(solution)/shard_map/ppermute | solution.py:38
  8.0 0.5 collective-permute-start.2
  8.5 0.1 collective-permute-start.1
  8.7 0.0 copy-done.7
  8.7 0.0 copy-done.2
  8.7 0.0 copy-done.4
  8.7 1.9 %conv_tables.1 = (bf16[2048,256]{1,0:T(8,128)(2,1)S(1)}, f32[512,128]{1,0:T(8,128)S(1)}, bf16[128,256]{1,0:T(8,128)(2,1)S(1)}) custom-call(f32[16,9]{1,0:T(8,128)S(1)} %copy-done.4, f32[1,16]{1,0:T(1,128)S(1)} %bitcast.16, bf16[64,32]{1,0:T(8,128)(2,1)S(1)} %bitcast.13), custom_call_target="tpu_custom_call" | custom-call | tf_op jit(solution)/shard_map/conv_tables/pallas_call | solution.py:125
  10.5 0.0 collective-permute-done.3
  10.6 1.4 %collective-permute-done.2 = bf16[64,256]{1,0:T(8,128)(2,1)S(1)} collective-permute-done((bf16[64,256]{1,0:T(8,128)(2,1)S(1)}, bf16[64,256]{1,0:T(8,128)(2,1)S(1)}, u32[]{:S(2)}, u32[]{:S(2)}) %collective-permute-start.2) | collective-permute-done | bytes 32800 | tf_op jit(solution)/shard_map/ppermute | solution.py:38
  11.9 0.5 collective-permute-done.1
  12.5 3.7 %collective-permute-start.6 = (bf16[64,256]{1,0:T(8,128)(2,1)S(1)}, bf16[64,256]{1,0:T(8,128)(2,1)S(1)}, u32[]{:S(2)}, u32[]{:S(2)}) collective-permute-start(bf16[64,256]{1,0:T(8,128)(2,1)S(1)} %add_add_fusion.1), channel_id=1, source_target_pairs={{0,24},{1,25},{2,26},{3,27},{4,28},{5,29},{6,30},{7,31},{8,16},{9,... | collective-permute-start | bytes 98312 | tf_op jit(solution)/shard_map/ppermute | solution.py:38
  16.1 0.0 collective-permute-start.5
  16.1 0.8 %collective-permute-start.4 = (bf16[64,256]{1,0:T(8,128)(2,1)S(1)}, bf16[64,256]{1,0:T(8,128)(2,1)S(1)}, u32[]{:S(2)}, u32[]{:S(2)}) collective-permute-start(bf16[64,256]{1,0:T(8,128)(2,1)S(1)} %add_add_fusion.1), channel_id=1, source_target_pairs={{0,16},{1,17},{2,18},{3,19},{4,20},{5,21},{6,22},{7,23},{8,24},{9,... | collective-permute-start | bytes 98312 | tf_op jit(solution)/shard_map/ppermute | solution.py:38
  16.9 0.0 copy-done.8
  16.9 0.2 copy.13
  17.1 0.0 copy-start.1
  17.1 0.7 %order_proj.1.refs_6_ = bf16[2048,512]{1,0:T(8,128)(2,1)S(1)} custom-call(bf16[2048,512]{1,0:T(8,128)(2,1)S(1)} %bitcast.12), custom_call_target="tpu_custom_call" | custom-call | tf_op jit(solution)/shard_map/order_proj/pallas_call | solution.py:165
  17.8 0.5 collective-permute-done.6
  18.3 1.7 %collective-permute-done.5 = bf16[64,256]{1,0:T(8,128)(2,1)S(1)} collective-permute-done((bf16[64,256]{1,0:T(8,128)(2,1)S(1)}, bf16[64,256]{1,0:T(8,128)(2,1)S(1)}, u32[]{:S(2)}, u32[]{:S(2)}) %collective-permute-start.5) | collective-permute-done | bytes 32800 | tf_op jit(solution)/shard_map/ppermute | solution.py:38
  20.0 0.9 %collective-permute-done.4 = bf16[64,256]{1,0:T(8,128)(2,1)S(1)} collective-permute-done((bf16[64,256]{1,0:T(8,128)(2,1)S(1)}, bf16[64,256]{1,0:T(8,128)(2,1)S(1)}, u32[]{:S(2)}, u32[]{:S(2)}) %collective-permute-start.4) | collective-permute-done | bytes 32800 | tf_op jit(solution)/shard_map/ppermute | solution.py:38
  21.0 0.0 copy-start.3
  21.0 0.0 copy-start.5
  21.0 0.0 copy-start.6
  21.0 0.1 collective-permute-start.7
  21.1 1.2 %collective-permute-done.7.refs_1_ = bf16[64,256]{1,0:T(8,128)(2,1)S(1)} collective-permute-done((bf16[64,256]{1,0:T(8,128)(2,1)S(1)}, bf16[64,256]{1,0:T(8,128)(2,1)S(1)}, u32[]{:S(2)}, u32[]{:S(2)}) %collective-permute-start.7) | collective-permute-done | bytes 32800 | tf_op jit(solution)/shard_map/ppermute | solution.py:397
  22.3 0.0 copy-done.1
  22.3 7.6 %frame_rows.1 = bf16[128,512]{1,0:T(8,128)(2,1)S(1)} custom-call(bf16[64,256]{1,0:T(8,128)(2,1)S(1)} %add_add_fusion.refs_0_, bf16[64,256]{1,0:T(8,128)(2,1)S(1)} %collective-permute-done.7.refs_1_, bf16[1,4096,256]{2,1,0:T(8,128)(2,1)S(1)} %copy-done.1, bf16[2048,256]{1,0:T(8,128)(2,1)S(1)} %get-tuple-element.33.refs_3_, ...), custom_call_target="tpu_custom_call" | custom-call | tf_op jit(solution)/shard_map/frame_rows/pallas_call | solution.py:253
  30.0 11.4 %all_to_all.20 = bf16[32,4,512]{2,1,0:T(4,128)(2,1)S(1)} all-to-all(bf16[32,4,512]{2,1,0:T(4,128)(2,1)S(1)} %all_to_all.13), channel_id=1, replica_groups=mesh['groups'=1,'frames'=32] {'frames'}, dimensions={0} | all-to-all | bytes 262144 | tf_op jit(solution)/shard_map/all_to_all | solution.py:399
  41.4 0.0 copy-done.3
  41.4 0.0 copy-done.5
  41.4 0.0 copy-done.6
  41.4 4.4 %mixer.1 = bf16[128,512]{1,0:T(8,128)(2,1)S(1)} custom-call(bf16[128,512]{1,0:T(8,128)(2,1)S(1)} %all_to_all.15.refs_0_, s32[1,32]{1,0:T(1,128)S(1)} %bitcast.15, f32[2,2,512]{2,1,0:T(2,128)S(1)} %copy-done.5, f32[3,2,512]{2,1,0:T(2,128)S(1)} %bitcast.14, bf16[2,512,2048]{2,1,0:T(8,128)(2,1)} %refs_4_.1, bf16[2,2048,512]{2,1,0:T(8,128)(2,1)} %refs_5_.1), custom_call_target="tpu_custom_call" | custom-call | tf_op jit(solution)/shard_map/mixer/pallas_call | solution.py:339
  45.9 10.0 %all_to_all.21 = bf16[32,4,512]{2,1,0:T(4,128)(2,1)S(1)} all-to-all(bf16[32,4,512]{2,1,0:T(4,128)(2,1)S(1)} %all_to_all.16), channel_id=1, replica_groups=mesh['groups'=1,'frames'=32] {'frames'}, dimensions={0} | all-to-all | bytes 262144 | tf_op jit(solution)/shard_map/all_to_all | solution.py:402
  55.9 0.7 %broadcast_in_dim.8 = bf16[1,128,512]{2,1,0:T(8,128)(2,1)} reshape(bf16[32,4,512]{2,1,0:T(4,128)(2,1)S(1)} %all_to_all.21) | data formatting | bytes 262144 | tf_op jit(solution)/shard_map/broadcast_in_dim | solution.py:403
  (6 shorter events, 0.1 us)
Async XLA Ops:
  0.0 8.7 %copy-start.7 = (f32[16]{0:T(128)S(1)}, f32[16]{0:T(128)}, u32[]{:S(2)}) copy-start(f32[16]{0:T(128)} %param.17) | copy-start | bytes 196
  0.7 1.6 %copy-start = (bf16[1,4096,256]{2,1,0:T(8,128)(2,1)S(1)}, bf16[1,4096,256]{2,1,0:T(8,128)(2,1)}, u32[]{:S(2)}) copy-start(bf16[1,4096,256]{2,1,0:T(8,128)(2,1)} %refs_2_.2) | copy-start | bytes 6291460
  2.3 6.4 %copy-start.2 = (bf16[32,16,2,2]{0,3,2,1:T(2,128)(2,1)S(1)}, bf16[32,16,2,2]{0,3,2,1:T(2,128)(2,1)}, u32[]{:S(2)}) copy-start(bf16[32,16,2,2]{0,3,2,1:T(2,128)(2,1)} %param.18) | copy-start | bytes 12292
  2.3 6.4 %copy-start.4 = (f32[16,9]{1,0:T(8,128)S(1)}, f32[16,9]{1,0:T(8,128)}, u32[]{:S(2)}) copy-start(f32[16,9]{1,0:T(8,128)} %refs_0_) | copy-start | bytes 1732
  2.3 14.6 %copy-start.8 = (bf16[2048,512]{1,0:T(8,128)(2,1)S(1)}, bf16[2048,512]{1,0:T(8,128)(2,1)}, u32[]{:S(2)}) copy-start(bf16[2048,512]{1,0:T(8,128)(2,1)} %param.19) | copy-start | bytes 6291460
  2.8 1.4 %collective-permute-start = (bf16[64,256]{1,0:T(8,128)(2,1)S(1)}, bf16[64,256]{1,0:T(8,128)(2,1)S(1)}, u32[]{:S(2)}, u32[]{:S(2)}) collective-permute-start(bf16[64,256]{1,0:T(8,128)(2,1)S(1)} %get-tuple-element.22), channel_id=1, source_target_pairs={{0,1},{1,0},{2,3},{3,2},{4,5},{5,4},{6,7},{7,6},{8,9},{9,8},{10,11... | collective-permute-start | bytes 98312 | tf_op jit(solution)/shard_map/ppermute | solution.py:387
  4.2 6.4 %collective-permute-start.3 = (bf16[64,256]{1,0:T(8,128)(2,1)S(1)}, bf16[64,256]{1,0:T(8,128)(2,1)S(1)}, u32[]{:S(2)}, u32[]{:S(2)}) collective-permute-start(bf16[64,256]{1,0:T(8,128)(2,1)S(1)} %add.21), channel_id=1, source_target_pairs={{0,6},{1,7},{2,4},{3,5},{4,2},{5,3},{6,0},{7,1},{8,14},{9,15},{10,... | collective-permute-start | bytes 98312 | tf_op jit(solution)/shard_map/ppermute | solution.py:38
  8.0 3.9 %collective-permute-start.2 = (bf16[64,256]{1,0:T(8,128)(2,1)S(1)}, bf16[64,256]{1,0:T(8,128)(2,1)S(1)}, u32[]{:S(2)}, u32[]{:S(2)}) collective-permute-start(bf16[64,256]{1,0:T(8,128)(2,1)S(1)} %add.21), channel_id=1, source_target_pairs={{0,4},{1,5},{2,6},{3,7},{4,0},{5,1},{6,2},{7,3},{8,12},{9,13},{10,... | collective-permute-start | bytes 98312 | tf_op jit(solution)/shard_map/ppermute | solution.py:38
  8.5 3.9 %collective-permute-start.1 = (bf16[64,256]{1,0:T(8,128)(2,1)S(1)}, bf16[64,256]{1,0:T(8,128)(2,1)S(1)}, u32[]{:S(2)}, u32[]{:S(2)}) collective-permute-start(bf16[64,256]{1,0:T(8,128)(2,1)S(1)} %add.21), channel_id=1, source_target_pairs={{0,2},{1,3},{2,0},{3,1},{4,6},{5,7},{6,4},{7,5},{8,10},{9,11},{10,... | collective-permute-start | bytes 98312 | tf_op jit(solution)/shard_map/ppermute | solution.py:38
  12.5 5.9 %collective-permute-start.6 = (bf16[64,256]{1,0:T(8,128)(2,1)S(1)}, bf16[64,256]{1,0:T(8,128)(2,1)S(1)}, u32[]{:S(2)}, u32[]{:S(2)}) collective-permute-start(bf16[64,256]{1,0:T(8,128)(2,1)S(1)} %add_add_fusion.1), channel_id=1, source_target_pairs={{0,24},{1,25},{2,26},{3,27},{4,28},{5,29},{6,30},{7,31},{8,16},{9,... | collective-permute-start | bytes 98312 | tf_op jit(solution)/shard_map/ppermute | solution.py:38
  16.1 3.9 %collective-permute-start.5 = (bf16[64,256]{1,0:T(8,128)(2,1)S(1)}, bf16[64,256]{1,0:T(8,128)(2,1)S(1)}, u32[]{:S(2)}, u32[]{:S(2)}) collective-permute-start(bf16[64,256]{1,0:T(8,128)(2,1)S(1)} %add_add_fusion.1), channel_id=1, source_target_pairs={{0,8},{1,9},{2,10},{3,11},{4,12},{5,13},{6,14},{7,15},{8,0},{9,1},... | collective-permute-start | bytes 98312 | tf_op jit(solution)/shard_map/ppermute | solution.py:38
  16.1 4.8 %collective-permute-start.4 = (bf16[64,256]{1,0:T(8,128)(2,1)S(1)}, bf16[64,256]{1,0:T(8,128)(2,1)S(1)}, u32[]{:S(2)}, u32[]{:S(2)}) collective-permute-start(bf16[64,256]{1,0:T(8,128)(2,1)S(1)} %add_add_fusion.1), channel_id=1, source_target_pairs={{0,16},{1,17},{2,18},{3,19},{4,20},{5,21},{6,22},{7,23},{8,24},{9,... | collective-permute-start | bytes 98312 | tf_op jit(solution)/shard_map/ppermute | solution.py:38
  17.1 5.2 %copy-start.1 = (bf16[1,4096,256]{2,1,0:T(8,128)(2,1)S(1)}, bf16[1,4096,256]{2,1,0:T(8,128)(2,1)}, u32[]{:S(2)}) copy-start(bf16[1,4096,256]{2,1,0:T(8,128)(2,1)} %refs_2_.2) | copy-start | bytes 6291460
  21.0 20.4 %copy-start.3 = (f32[2,3,512]{2,0,1:T(2,128)S(1)}, f32[2,3,512]{2,0,1:T(2,128)}, u32[]{:S(2)}) copy-start(f32[2,3,512]{2,0,1:T(2,128)} %param.21) | copy-start | bytes 36868
  21.0 20.4 %copy-start.5 = (f32[2,2,512]{2,1,0:T(2,128)S(1)}, f32[2,2,512]{2,1,0:T(2,128)}, u32[]{:S(2)}) copy-start(f32[2,2,512]{2,1,0:T(2,128)} %refs_2_.3) | copy-start | bytes 24580
  21.0 20.4 %copy-start.6 = (s32[32]{0:T(128)S(1)}, s32[32]{0:T(128)}, u32[]{:S(2)}) copy-start(s32[32]{0:T(128)} %param.15) | copy-start | bytes 388
  21.0 1.3 %collective-permute-start.7 = (bf16[64,256]{1,0:T(8,128)(2,1)S(1)}, bf16[64,256]{1,0:T(8,128)(2,1)S(1)}, u32[]{:S(2)}, u32[]{:S(2)}) collective-permute-start(bf16[64,256]{1,0:T(8,128)(2,1)S(1)} %add_add_fusion.refs_0_), channel_id=1, source_target_pairs={{0,1},{1,0},{2,3},{3,2},{4,5},{5,4},{6,7},{7,6},{8,9},{9,8},{10,11... | collective-permute-start | bytes 98312 | tf_op jit(solution)/shard_map/ppermute | solution.py:397
